TPU v7x, 256 devices: a whole 4x4x8 slice. The times are simulated.
256 devices in a mesh: role: 2 (over y_lo), req: 8 (over x, core), ctx: 16 (over y_hi, z).
Axes of the slice: x: 4, y: 4 (y_hi: 2, y_lo: 2; y = y_hi * 2 + y_lo), z: 8, core: 2. Of those that a mesh axis runs over, the one named last changes fastest.
Arguments:
- query: bfloat16 [64, 16384], P('req', 'role'), may hold values from -12 to 12
- cache_keys: bfloat16 [64, 2048, 1024], P('req', 'ctx', 'role'), may hold values from -6 to 6
- cache_values: bfloat16 [64, 2048, 1024], P('req', 'ctx', 'role'), may hold values from -6 to 6
- new_keys: bfloat16 [64, 1024], P('req', 'role'), may hold values from -6 to 6
- new_values: bfloat16 [64, 1024], P('req', 'role'), may hold values from -6 to 6
- lengths: int32 [64], P('req'), may hold values from 512 to 2048, as said below
- residual_in: bfloat16 [64, 8192], P(None, 'req'), may hold values from -24 to 24
- out_proj: bfloat16 [16384, 8192], P(('role', 'ctx'), 'req'), may hold values from -1.5 to 1.5
- norm_gain: float32 [8192], replicated, may hold values from 0.1 to 1.9
- adapter_down: bfloat16 [8192, 256], P('req'), may hold values from -0.0625 to 0.0625
- tenant_adapter_up_matrix: bfloat16 [256, 32768], P(None, ('role', 'req', 'ctx')), may hold values from -1.5 to 1.5
- tenant: int32 [64], replicated, may hold values from 0 to 15
- w_gate: bfloat16 [8192, 32768], P(None, ('role', 'req', 'ctx')), may hold values from -0.0625 to 0.0625
- w_up: bfloat16 [8192, 32768], P(None, ('role', 'req', 'ctx')), may hold values from -0.0625 to 0.0625
- w_down: bfloat16 [32768, 8192], P(('role', 'req', 'ctx')), may hold values from -0.125 to 0.125
Outputs:
- hidden_out: bfloat16 [64, 8192], P('req', ('role', 'ctx'))
Inputs may be any that keep to these rules, and one draw needn't show every extreme that they name: `lengths`: each request has between a quarter of the cache and all of it in use; some request uses all 2048 positions.
All inputs are finite; a program needn't handle non-finite values.
Results may differ from a plain program's by a relative error of at most 0.0058.
Values may be sent and summed in bfloat16 or wider, within the bound.
A program may use at most 64 MiB of HBM per device.

v0:
```python
import math

import jax
import jax.numpy as jnp
from jax import lax
from jax.sharding import PartitionSpec as P

HD = 128
RANK = 16


epsilon = 1e-05
low_rank_weight = 2.0
masked_lower_limit = -1e30


def shards(
    query,
    cache_keys,
    cache_values,
    new_keys,
    new_values,
    lengths,
    residual_in,
    out_proj,
    norm_gain,
    adapter_down,
    tenant_adapter_up_matrix,
    tenant,
    w_gate,
    w_up,
    w_down,
):
    rows_here = query.shape[0]
    span = cache_keys.shape[1]
    kv_local = new_keys.shape[1] // HD
    heads_local = query.shape[1] // HD
    group_size = heads_local // kv_local
    factor = 1.0 / math.sqrt(HD)
    grouped = query.reshape(rows_here, kv_local, group_size, HD)
    keys_local = cache_keys.reshape(rows_here, span, kv_local, HD)
    values_float = cache_values.reshape(rows_here, span, kv_local, HD).astype(jnp.float32)
    scores = (
        jnp.einsum("rkgd,rpkd->rkgp", grouped, keys_local, preferred_element_type=jnp.float32)
        * factor
    )
    position = lax.axis_index("ctx") * span + jnp.arange(span)
    usable = (position[None, :] < lengths[:, None])[:, None, None, :]
    masked = jnp.where(usable, scores, masked_lower_limit)
    fresh_token_score = (
        jnp.einsum(
            "rkgd,rkd->rkg",
            grouped,
            new_keys.reshape(rows_here, kv_local, HD),
            preferred_element_type=jnp.float32,
        )
        * factor
    )
    fresh_value = new_values.reshape(rows_here, kv_local, 1, HD).astype(jnp.float32)
    local_peak = jnp.max(masked, axis=-1)
    cached_peak = lax.pmax(local_peak, "ctx")
    highest = jnp.maximum(cached_peak, fresh_token_score)
    weights = jnp.where(usable, jnp.exp(masked - highest[..., None]), 0.0)
    partial_sum = jnp.sum(weights, axis=-1)
    partial_acc = jnp.einsum(
        "rkgp,rpkd->rkgd", weights, values_float, precision=lax.Precision.HIGHEST
    )
    denominator, numerator = lax.psum((partial_sum, partial_acc), "ctx")
    self_weight = jnp.exp(fresh_token_score - highest)
    denominator = denominator + self_weight
    numerator = numerator + self_weight[..., None] * fresh_value
    attention = (
        (numerator / denominator[..., None])
        .reshape(rows_here, heads_local * HD)
        .astype(jnp.bfloat16)
    )
    slab_width = out_proj.shape[0]
    attn_slab = lax.dynamic_slice_in_dim(
        attention, lax.axis_index("ctx") * slab_width, slab_width, 1
    )
    partial_proj = jnp.dot(
        lax.all_gather(attn_slab, "req", axis=0, tiled=True),
        out_proj,
        preferred_element_type=jnp.float32,
    )
    projected = lax.psum(partial_proj, ("role", "ctx"))
    stream_block = (residual_in.astype(jnp.float32) + projected).astype(jnp.bfloat16)
    stream = lax.all_gather(stream_block, "req", axis=1, tiled=True)
    widened = stream.astype(jnp.float32)
    inverse = lax.rsqrt(jnp.mean(widened * widened, axis=-1, keepdims=True) + epsilon)
    normed = (widened * inverse * norm_gain).astype(jnp.bfloat16)
    width_block = adapter_down.shape[0]
    normed_block = lax.dynamic_slice_in_dim(
        normed, lax.axis_index("req") * width_block, width_block, 1
    )
    adapter_mid = lax.psum(
        jnp.dot(normed_block, adapter_down, preferred_element_type=jnp.float32), "req"
    )
    owners = jnp.arange(adapter_mid.shape[1]) // RANK
    picked_tenant = jnp.where(tenant[:, None] == owners[None, :], adapter_mid, 0.0).astype(
        jnp.bfloat16
    )
    gate = jnp.dot(normed, w_gate, preferred_element_type=jnp.float32)
    up_projection_share = jnp.dot(normed, w_up, preferred_element_type=jnp.float32)
    up_projection_share = up_projection_share + low_rank_weight * jnp.dot(
        picked_tenant, tenant_adapter_up_matrix, preferred_element_type=jnp.float32
    )
    hidden = (jax.nn.silu(gate) * up_projection_share).astype(jnp.bfloat16)
    role_count = lax.axis_size("role")
    ctx_count = lax.axis_size("ctx")
    column_width = stream.shape[1] // (role_count * ctx_count)
    column_index = lax.axis_index("role") * ctx_count + lax.axis_index("ctx")
    down_terms = jnp.dot(hidden, w_down, preferred_element_type=jnp.float32)
    narrowed = lax.psum_scatter(down_terms, ("role", "ctx"), scatter_dimension=1, tiled=True)
    reduced = lax.psum_scatter(narrowed, "req", scatter_dimension=0, tiled=True)
    own_stream = lax.dynamic_slice(
        widened,
        (lax.axis_index("req") * rows_here, column_index * column_width),
        (rows_here, column_width),
    )
    return (own_stream + reduced).astype(jnp.bfloat16)


def solution(mesh):
    placed = (
        P("req", "role"),
        P("req", "ctx", "role"),
        P("req", "ctx", "role"),
        P("req", "role"),
        P("req", "role"),
        P("req"),
        P(None, "req"),
        P(("role", "ctx"), "req"),
        P(),
        P("req", None),
        P(None, ("role", "req", "ctx")),
        P(),
        P(None, ("role", "req", "ctx")),
        P(None, ("role", "req", "ctx")),
        P(("role", "req", "ctx"), None),
    )
    return jax.shard_map(
        shards, mesh=mesh, in_specs=placed, out_specs=P("req", ("role", "ctx")), check_vma=False
    )
```

profile of v0, /device:TPU:1, one launch (start us, length us, event | category | flops | bytes accessed | tf_op | source)
XLA Modules:
  0.0 650.8 jit_solution(17683983610579134331)
XLA Ops:
  6.5 0.9 broadcast_compare_fusion
  7.4 2.0 fusion.40
  9.5 67.0 %pmax.7 = f32[8,4,16]{2,1,0:T(4,128)S(1)} all-reduce(f32[8,4,16]{2,1,0:T(4,128)S(1)} %get-tuple-element.7), channel_id=1, replica_groups=mesh['role'=2,'req'=8,'ctx'=16] {'ctx'}, use_global_device_ids=true, to_apply=%region_1.2 | all-reduce | flops 512 | bytes 4096 | tf_op jit(solution)/shard_map/pmax | solution.py:61
  76.5 1.1 fusion.16
  77.6 2.9 fusion.5
  80.9 58.8 %psum.29 = f32[8,4,16]{2,1,0:T(4,128)S(1)} all-reduce(f32[8,4,16]{2,1,0:T(4,128)S(1)} %fusion.10), channel_id=1, replica_groups=mesh['role'=2,'req'=8,'ctx'=16] {'ctx'}, use_global_device_ids=true, to_apply=%region_4.5 | all-reduce | flops 512 | bytes 4096 | tf_op jit(solution)/shard_map/psum | solution.py:68
  139.7 95.0 %all-reduce.3.cloned.1.call-done = f32[8,4,16,128]{3,2,1,0:T(8,128)} async-done(((f32[8,4,16,128]{3,2,1,0:T(8,128)}), f32[8,4,16,128]{3,2,1,0:T(8,128)}) %all-reduce.3.cloned.1.call-update) | async-done | bytes 262160 | tf_op jit(solution)/shard_map/psum | solution.py:68
  234.7 1.2 divide_convert_fusion
  236.0 23.3 %all_gather.6 = bf16[64,512]{1,0:T(8,128)(2,1)S(1)} all-gather(bf16[8,512]{1,0:T(8,128)(2,1)S(1)} %constant_dynamic-slice_fusion), channel_id=1, replica_groups=mesh['role'=2,'req'=8,'ctx'=16] {'req'}, dimensions={0}, use_global_device_ids=true | all-gather | bytes 73728 | tf_op jit(solution)/shard_map/all_gather | solution.py:82
  259.3 1.0 fusion.41
  260.4 136.2 %all-reduce.5.cloned.1.call-done = f32[64,1024]{1,0:T(8,128)} async-done(((f32[64,1024]{1,0:T(8,128)}), f32[64,1024]{1,0:T(8,128)}) %all-reduce.5.cloned.1.call-update) | async-done | bytes 262160 | tf_op jit(solution)/shard_map/psum | solution.py:86
  396.6 1.6 add_convert_fusion
  398.3 28.0 %all-gather.2.cloned.1.call-done = bf16[64,8192]{1,0:T(8,128)(2,1)} async-done(((bf16[64,1024]{1,0:T(8,128)(2,1)}), bf16[64,8192]{1,0:T(8,128)(2,1)}) %all-gather.2.cloned.1.call-update) | async-done | bytes 1048592 | tf_op jit(solution)/shard_map/all_gather | solution.py:88
  426.3 1.5 multiply_reduce_fusion
  427.9 1.5 multiply_convert_fusion
  429.4 1.3 fusion.11
  430.7 21.4 %psum.31 = bf16[64,256]{1,0:T(8,128)(2,1)S(1)} all-reduce(f32[64,256]{1,0:T(8,128)S(1)} %fusion.11), channel_id=1, replica_groups=mesh['role'=2,'req'=8,'ctx'=16] {'req'}, use_global_device_ids=true, to_apply=%region_7.8 | all-reduce | flops 16384 | bytes 98304 | tf_op jit(solution)/shard_map/psum | solution.py:96
  452.1 2.2 fusion.42
  454.4 0.5 fusion.43
  455.2 2.0 fusion.4
  457.3 130.0 %reduce-scatter.3.cloned.1.call-done = f32[64,256]{1,0:T(8,128)} async-done(((f32[64,8192]{1,0:T(8,128)}), f32[64,256]{1,0:T(8,128)}) %reduce-scatter.3.cloned.1.call-update) | async-done | bytes 65552 | tf_op jit(solution)/shard_map/reduce_scatter | solution.py:114
  587.3 1.5 convert_element_type.45
  588.8 54.1 %reduce-scatter.5.cloned.1.call-done = f32[8,256]{1,0:T(8,128)} async-done(((f32[64,256]{1,0:T(8,128)}), f32[8,256]{1,0:T(8,128)}) %reduce-scatter.5.cloned.1.call-update) | async-done | bytes 8208 | tf_op jit(solution)/shard_map/reduce_scatter | solution.py:115
  642.9 1.3 add_convert_fusion.1
  (38 shorter events, 1.1 us)
Async XLA Ops:
  6.5 448.4 %copy-start = (bf16[128,8192]{1,0:T(8,128)(2,1)S(1)}, bf16[128,8192]{1,0:T(8,128)(2,1)}, u32[]{:S(2)}) copy-start(bf16[128,8192]{1,0:T(8,128)(2,1)} %param.29) | copy-start | bytes 6291460
  6.5 74.0 %copy-start.7 = (bf16[8,512]{1,0:T(8,128)(2,1)S(1)}, bf16[8,512]{1,0:T(8,128)(2,1)}, u32[]{:S(2)}) copy-start(bf16[8,512]{1,0:T(8,128)(2,1)} %param.19) | copy-start | bytes 24580
  6.5 228.1 %all-reduce.3.cloned.1.call-start = ((), (), s32[]{:S(2)}) async-start(), calls=%async_computation.2 | async-start | bytes 524288 | tf_op jit(solution)/shard_map/psum | solution.py:68
  9.5 249.8 %copy-start.3 = (bf16[512,1024]{1,0:T(8,128)(2,1)S(1)}, bf16[512,1024]{1,0:T(8,128)(2,1)}, u32[]{:S(2)}) copy-start(bf16[512,1024]{1,0:T(8,128)(2,1)} %param.22) | copy-start | bytes 3145732
  80.5 316.1 %all-reduce.5.cloned.1.call-start = ((), (), s32[]{:S(2)}) async-start(), calls=%async_computation.3 | async-start | bytes 524288 | tf_op jit(solution)/shard_map/psum | solution.py:86
  80.9 315.7 %copy-start.4 = (bf16[64,1024]{1,0:T(8,128)(2,1)S(1)}, bf16[64,1024]{1,0:T(8,128)(2,1)}, u32[]{:S(2)}) copy-start(bf16[64,1024]{1,0:T(8,128)(2,1)} %param.21) | copy-start | bytes 393220
  139.7 288.2 %copy-start.6 = (f32[8192]{0:T(1024)S(1)}, f32[8192]{0:T(1024)}, u32[]{:S(2)}) copy-start(f32[8192]{0:T(1024)} %param.23) | copy-start | bytes 98308
  260.3 166.0 %all-gather.2.cloned.1.call-start = ((), (), s32[]{:S(2)}) async-start(), calls=%async_computation.4 | async-start | bytes 1179648 | tf_op jit(solution)/shard_map/all_gather | solution.py:88
  398.3 189.0 %reduce-scatter.3.cloned.1.call-start = ((), (), s32[]{:S(2)}) async-start(), calls=%async_computation.5 | async-start | bytes 2162688 | tf_op jit(solution)/shard_map/reduce_scatter | solution.py:114
  452.1 2.2 copy-start.2
  454.4 0.8 copy-start.5
  454.4 0.8 copy-start.8
  457.2 130.1 %copy-start.1 = (bf16[64,8192]{1,0:T(8,128)(2,1)S(1)}, bf16[64,8192]{1,0:T(8,128)(2,1)}, u32[]{:S(2)}) copy-start(bf16[64,8192]{1,0:T(8,128)(2,1)} %all-gather.2.cloned.1.call-done) | copy-start | bytes 3145732
  457.2 185.7 %reduce-scatter.5.cloned.1.call-start = ((), (), s32[]{:S(2)}) async-start(), calls=%async_computation.6 | async-start | bytes 73728 | tf_op jit(solution)/shard_map/reduce_scatter | solution.py:115
Sparse Core Ops, SparseCore 0:
  80.7 153.9 all-reduce.2
  260.4 136.1 all-reduce.4
  398.6 27.7 all-gather.1
  457.3 129.9 reduce-scatter.2
  589.6 53.2 reduce-scatter.4
where the time goes:
time: 653 us; the launch traced here: 651 us
  waiting for transfers between devices  443 us (68%)
  blocking collectives  171 us (26%)
  between operations  13.4 us (2%)
  matrix products  13 us (2%)
  other arithmetic  9.85 us (2%)
    psum x1, waiting for transfers between devices, shards(): projected = lax.psum(partial_proj, ('role', 'ctx'))  136 us
    reduce_scatter x1, waiting for transfers between devices, shards(): lax.psum_scatter(down_terms, ('role', 'ctx'), scatter_dimension=1, tiled=...  130 us
    psum x1, waiting for transfers between devices, shards(): denominator, numerator = lax.psum((partial_sum, partial_acc), 'ctx')  95 us
    pmax x1, blocking collectives, shards(): cached_peak = lax.pmax(local_peak, 'ctx')  67 us
    psum x1, blocking collectives, shards(): denominator, numerator = lax.psum((partial_sum, partial_acc), 'ctx')  58.8 us
    reduce_scatter x1, waiting for transfers between devices, shards(): reduced = lax.psum_scatter(narrowed, 'req', scatter_dimension=0, tiled=True)  54.1 us
    all_gather x1, waiting for transfers between devices, shards(): stream = lax.all_gather(stream_block, 'req', axis=1, tiled=True)  28 us
    all_gather x1, blocking collectives, shards(): lax.all_gather(attn_slab, 'req', axis=0, tiled=True)  23.3 us
  transfers between devices with their start and end apart: 5, of which 5 were waited for; matrix products, arithmetic and copies ran while one was open for 0% of the time, Pallas kernels for 0%

commit v1 on v0

v1 whole, which is shorter than its diff:
```python
import functools
import math

import jax
import jax.numpy as jnp
from jax import lax
from jax.experimental import pallas as pl
from jax.experimental.pallas import tpu as pltpu
from jax.sharding import PartitionSpec as P

MESH = pl.DeviceIdType.MESH
F32 = jnp.float32
BF16 = jnp.bfloat16
HD = 128
EPS = 1e-05
LOW = -1e30
NT = (((1,), (1,)), ((), ()))


def rcopy(src, dst, ssem, rsem, dev):
    return pltpu.make_async_remote_copy(
        src_ref=src, dst_ref=dst, send_sem=ssem, recv_sem=rsem, device_id=dev, device_id_type=MESH
    )


def loop(lo, hi, body):
    def step(i, carry):
        body(i)
        return carry

    lax.fori_loop(lo, hi, step, 0)


def kernel(
    stop,
    q_h, ck_h, cv_h, nk_h, nv_h, len_s, res_h, wo_h, gain_h, ad_h, tu_h, ten_s, wg_h, wu_h, wd_h,
    out_ref,
    q_v, ck_v, cv_v, nk_v, nv_v, res_v, wo_v, gain_v, ad_v, tu_v, wgu_v, wd_v,
    qrows, acc_s, stat_s, racc, rstat, rt_v,
    ogath, psend, rpart, xs, ad_s, rad, dbuf, rcore, r1, rx, r2, ry, r3, rz,
    lsem,
    sa_s, sa_r, ss_s, ss_r, so_s, so_r, sp_s, sp_r, sz_s, sz_r, sy_s, sy_r, sx_s, sx_r, sc_s, sc_r,
    sd_s, sd_r, e_c, e_x, e_y, e_z,
):
    role = lax.axis_index("role")
    req = lax.axis_index("req")
    ctx = lax.axis_index("ctx")
    x = lax.div(req, 2)
    core = lax.rem(req, 2)
    yhi = lax.div(ctx, 8)
    z = lax.rem(ctx, 8)
    y = yhi * 2 + role
    yz = role * 16 + ctx
    me = (role, req, ctx)

    def at_yz(i):
        return (lax.div(i, 16), req, lax.rem(i, 16))

    def at_req(i):
        return (role, i, ctx)

    def at_y(i):
        return (lax.rem(i, 2), req, lax.div(i, 2) * 8 + z)

    def at_z(i):
        return (role, req, yhi * 8 + i)

    local = [
        pltpu.make_async_copy(q_h, q_v, lsem.at[0]),
        pltpu.make_async_copy(ck_h, ck_v, lsem.at[1]),
        pltpu.make_async_copy(cv_h, cv_v, lsem.at[2]),
        pltpu.make_async_copy(nk_h, nk_v, lsem.at[3]),
        pltpu.make_async_copy(nv_h, nv_v, lsem.at[4]),
        pltpu.make_async_copy(wo_h, wo_v, lsem.at[5]),
        pltpu.make_async_copy(
            res_h.at[pl.ds(pl.multiple_of(y * 16, 16), 16), pl.ds(pl.multiple_of(z * 128, 128), 128)],
            res_v, lsem.at[6],
        ),
        pltpu.make_async_copy(gain_h, gain_v, lsem.at[7]),
        pltpu.make_async_copy(ad_h, ad_v, lsem.at[8]),
        pltpu.make_async_copy(tu_h, tu_v, lsem.at[9]),
        pltpu.make_async_copy(wg_h, wgu_v.at[:, pl.ds(0, 128)], lsem.at[10]),
        pltpu.make_async_copy(wu_h, wgu_v.at[:, pl.ds(128, 128)], lsem.at[11]),
        pltpu.make_async_copy(wd_h, wd_v, lsem.at[12]),
    ]
    for c in local:
        c.start()

    barrier = pltpu.get_barrier_semaphore()
    loop(1, 32, lambda o: pl.semaphore_signal(
        barrier, inc=1, device_id=at_yz(lax.rem(yz + o, 32)), device_id_type=MESH))
    loop(1, 8, lambda o: pl.semaphore_signal(
        barrier, inc=1, device_id=at_req(lax.rem(req + o, 8)), device_id_type=MESH))

    factor = 1.0 / math.sqrt(HD)
    sub = lax.broadcasted_iota(jnp.int32, (8, 128), 0)
    lane = lax.broadcasted_iota(jnp.int32, (8, 128), 1)
    lens = jnp.zeros((8, 128), jnp.int32)
    for r in range(8):
        lens = jnp.where(sub == r, len_s[r], lens)
    usable = (ctx * 128 + lane < lens)[None]
    rowmod = lax.broadcasted_iota(jnp.int32, (16, 8, 128), 1)
    stat_lane = lax.broadcasted_iota(jnp.int32, (128, 128), 1)
    local[0].wait()
    local[1].wait()
    local[2].wait()
    stat = jnp.zeros((128, 128), F32)
    for k in range(4):
        qk = jnp.concatenate(
            [q_v[:, (k * 16 + g) * 128:(k * 16 + g + 1) * 128].astype(F32) for g in range(16)], axis=0)
        qrows[k * 128:(k + 1) * 128, :] = qk
        kk = ck_v[:, :, k * 128:(k + 1) * 128].reshape(1024, 128)
        full = lax.dot_general(qk.astype(BF16), kk, NT, preferred_element_type=F32)
        sc = jnp.zeros((16, 8, 128), F32)
        for r in range(8):
            sc = jnp.where(rowmod == r, full[:, r * 128:(r + 1) * 128].reshape(16, 8, 128), sc)
        sc = jnp.where(usable, sc * factor, LOW)
        top = jnp.max(sc, axis=-1, keepdims=True)
        w = jnp.where(usable, jnp.exp(sc - top), 0.0)
        wb = w.astype(BF16).astype(F32)
        tot = jnp.sum(wb, axis=-1, keepdims=True)
        big = jnp.concatenate(
            [jnp.where(rowmod == r, wb, 0.0).reshape(128, 128).astype(BF16) for r in range(8)], axis=1)
        vk = cv_v[:, :, k * 128:(k + 1) * 128].reshape(1024, 128)
        acc = jnp.dot(big, vk, preferred_element_type=F32)
        acc_s[4 * k:4 * k + 4] = acc.astype(BF16).reshape(4, 32, 128)
        stat = jnp.where(stat_lane == 2 * k, top.reshape(128, 1), stat)
        stat = jnp.where(stat_lane == 2 * k + 1, tot.reshape(128, 1), stat)
    stat_s[...] = stat.T[0:8, :]

    pl.semaphore_wait(barrier, 38)

    def acc_copy(o):
        c = lax.rem(ctx + o, 16)
        return rcopy(acc_s.at[c], racc.at[ctx], sa_s.at[o], sa_r.at[ctx], (role, req, c))

    def stat_copy(o):
        c = lax.rem(ctx + o, 16)
        return rcopy(stat_s, rstat.at[ctx], ss_s.at[o], ss_r.at[ctx], (role, req, c))

    def send_attn(o):
        acc_copy(o).start()
        stat_copy(o).start()

    loop(1, 16, send_attn)
    racc[ctx] = acc_s[ctx]
    rstat[ctx] = stat_s[...]

    kh = lax.div(ctx, 4)
    local[3].wait()
    local[4].wait()
    col = pl.ds(pl.multiple_of(kh * 128, 128), 128)
    q32 = qrows[pl.ds(pl.multiple_of(ctx * 32, 32), 32), :].reshape(4, 8, 128)
    nk = nk_v[:, col].astype(F32)
    nv = nv_v[:, col].astype(F32)
    s_self = (jnp.sum(q32 * nk[None], axis=-1, keepdims=True) * factor).reshape(32, 1)
    nv32 = jnp.broadcast_to(nv[None], (4, 8, 128)).reshape(32, 128)

    def wait_attn(o):
        c = lax.rem(ctx + o, 16)
        rcopy(acc_s.at[c], racc.at[c], sa_s.at[o], sa_r.at[c], me).wait_recv()
        rcopy(stat_s, rstat.at[c], ss_s.at[o], ss_r.at[c], me).wait_recv()

    loop(1, 16, wait_attn)
    rt_v[...] = rstat[...].reshape(128, 128).T
    st = rt_v[pl.ds(pl.multiple_of(lax.rem(ctx, 4) * 32, 32), 32), :]
    st = pltpu.roll(st, lax.rem(128 - 2 * kh, 128), 1)
    lane32 = lax.broadcasted_iota(jnp.int32, (32, 128), 1)
    first = lane32 % 8 == 0
    tops = jnp.where(first, st, -3e38)
    high = jnp.maximum(jnp.max(tops, axis=-1, keepdims=True), s_self)
    wgt = jnp.where(first, jnp.exp(tops - high), 0.0)
    w_self = jnp.exp(s_self - high)
    den = jnp.sum(wgt * pltpu.roll(st, 127, 1), axis=-1, keepdims=True) + w_self
    o_acc = w_self * nv32
    for s in range(16):
        o_acc = o_acc + wgt[:, 8 * s:8 * s + 1] * racc[s].astype(F32)
    ogath[req] = (o_acc / den).astype(BF16)

    def o_copy(o):
        return rcopy(ogath.at[req], ogath.at[req], so_s.at[o], so_r.at[req], at_req(lax.rem(req + o, 8)))

    loop(1, 8, lambda o: o_copy(o).start())

    def wait_o(o):
        c = lax.rem(req + o, 8)
        rcopy(ogath.at[c], ogath.at[c], so_s.at[o], so_r.at[c], me).wait_recv()

    loop(1, 8, wait_o)
    local[5].wait()
    og = ogath[...].astype(F32)
    attn = jnp.concatenate(
        [og[:, 8 * g:8 * g + 8, :].reshape(64, 128) for g in range(4)], axis=1).astype(BF16)
    proj = jnp.dot(attn, wo_v[...], preferred_element_type=F32)
    for yy in range(4):
        for zz in range(8):
            psend[yy, zz] = proj[16 * yy:16 * yy + 16, 128 * zz:128 * zz + 128].astype(BF16)

    def p_copy(o):
        d = lax.rem(yz + o, 32)
        rr, cc = lax.div(d, 16), lax.rem(d, 16)
        return rcopy(psend.at[lax.div(cc, 8) * 2 + rr, lax.rem(cc, 8)], rpart.at[yz],
                     sp_s.at[o], sp_r.at[yz], (rr, req, cc))

    loop(1, 32, lambda o: p_copy(o).start())
    rpart[yz] = psend[y, z]

    def wait_p(o):
        c = lax.rem(yz + o, 32)
        rcopy(rpart.at[c], rpart.at[c], sp_s.at[o], sp_r.at[c], me).wait_recv()

    loop(1, 32, wait_p)
    local[6].wait()
    piece = res_v[...].astype(F32) + jnp.sum(rpart[...].astype(F32), axis=0)
    rows_y = pl.ds(pl.multiple_of(y * 16, 16), 16)
    xs[req * 8 + z, rows_y, :] = piece.astype(BF16)

    def z_ref(i):
        return xs.at[req * 8 + i, rows_y]

    def z_copy(o):
        return rcopy(z_ref(z), z_ref(z), sz_s.at[o], sz_r.at[z], at_z(lax.rem(z + o, 8)))

    loop(1, 8, lambda o: z_copy(o).start())

    def wait_z(o):
        c = lax.rem(z + o, 8)
        rcopy(z_ref(c), z_ref(c), sz_s.at[o], sz_r.at[c], me).wait_recv()

    loop(1, 8, wait_z)

    def y_ref(i):
        return xs.at[pl.ds(req * 8, 8), pl.ds(pl.multiple_of(i * 16, 16), 16)]

    def y_copy(o):
        return rcopy(y_ref(y), y_ref(y), sy_s.at[o], sy_r.at[y], at_y(lax.rem(y + o, 4)))

    for o in range(1, 4):
        y_copy(o).start()
    for o in range(1, 4):
        c = lax.rem(y + o, 4)
        rcopy(y_ref(c), y_ref(c), sy_s.at[o], sy_r.at[c], me).wait_recv()

    def b_ref(b):
        return xs.at[pl.ds(b * 8, 8)]

    def x_copy(o):
        return rcopy(b_ref(req), b_ref(req), sx_s.at[o], sx_r.at[x], at_req(lax.rem(x + o, 4) * 2 + core))

    def c_copy(o):
        b = lax.rem(x + o, 4) * 2 + core
        return rcopy(b_ref(b), b_ref(b), sc_s.at[o], sc_r.at[lax.rem(x + o, 4)], at_req(x * 2 + 1 - core))

    for o in (1, 3, 2):
        x_copy(o).start()
    c_copy(0).start()
    local[7].wait()
    local[8].wait()
    local[10].wait()
    local[11].wait()

    def block(b):
        xb = xs[pl.ds(b * 8, 8)].astype(F32)
        sq = jnp.sum(jnp.sum(xb * xb, axis=0), axis=-1, keepdims=True)
        xg = xb * gain_v[pl.ds(pl.multiple_of(b * 8, 8), 8), :][:, None, :]
        xg = jnp.concatenate([xg[i] for i in range(8)], axis=1).astype(BF16)
        return sq, xg

    def gate_up(b, xg):
        rows = pl.ds(pl.multiple_of(b * 1024, 1024), 1024)
        return jnp.dot(xg, wgu_v[rows, :], preferred_element_type=F32)

    sq, xg = block(req)
    mid = jnp.dot(xg, ad_v[...], preferred_element_type=F32)
    owner = lax.div(lane, 16)
    tens = []
    packed = jnp.zeros((8, 128), F32)
    for i in range(8):
        t = jnp.zeros((8, 128), jnp.int32)
        for r in range(8):
            t = jnp.where(sub == r, ten_s[8 * i + r], t)
        tens.append(t)
        v = (jnp.where(owner == t, mid[8 * i:8 * i + 8, 0:128], 0.0)
             + jnp.where(owner + 8 == t, mid[8 * i:8 * i + 8, 128:256], 0.0))
        v = v + pltpu.roll(v, 64, 1)
        v = v + pltpu.roll(v, 32, 1)
        v = v + pltpu.roll(v, 16, 1)
        packed = jnp.where(owner == i, v, packed)
    ad_s[...] = packed

    def d_copy(o):
        return rcopy(ad_s, rad.at[req], sd_s.at[o], sd_r.at[req], at_req(lax.rem(req + o, 8)))

    loop(1, 8, lambda o: d_copy(o).start())
    rad[req] = packed
    gu = gate_up(req, xg)
    for o in (0, 1, 3, 2):
        xo = lax.rem(x + o, 4)
        if o > 0:
            b = xo * 2 + core
            rcopy(b_ref(b), b_ref(b), sx_s.at[o], sx_r.at[xo], me).wait_recv()
            c_copy(o).start()
            s1, xg = block(b)
            sq = sq + s1
            gu = gu + gate_up(b, xg)
        b = xo * 2 + 1 - core
        rcopy(b_ref(b), b_ref(b), sc_s.at[o], sc_r.at[xo], me).wait_recv()
        s1, xg = block(b)
        sq = sq + s1
        gu = gu + gate_up(b, xg)

    def wait_d(o):
        c = lax.rem(req + o, 8)
        rcopy(ad_s, rad.at[c], sd_s.at[o], sd_r.at[c], me).wait_recv()

    loop(1, 8, wait_d)
    inv = lax.rsqrt(sq * (1.0 / 8192.0) + EPS)
    allmid = jnp.sum(rad[...], axis=0)
    chosen = []
    for i in range(8):
        v = jnp.where(owner == i, allmid, 0.0)
        v = v + pltpu.roll(v, 64, 1)
        v = v + pltpu.roll(v, 32, 1)
        v = v + pltpu.roll(v, 16, 1)
        v = v * inv[8 * i:8 * i + 8]
        chosen.append(jnp.concatenate(
            [jnp.where(owner == tens[i], v, 0.0), jnp.where(owner + 8 == tens[i], v, 0.0)], axis=1))
    local[9].wait()
    lowrank = jnp.dot(jnp.concatenate(chosen, axis=0).astype(BF16), tu_v[...], preferred_element_type=F32)
    gate = gu[:, 0:128] * inv
    up = gu[:, 128:256] * inv + 2.0 * lowrank
    hid = (gate / (1.0 + jnp.exp(-gate)) * up).astype(BF16)

    local[12].wait()
    for p in range(32):
        rr, cc = p // 16, p % 16
        yy, zz = (cc // 8) * 2 + rr, cc % 8
        part = jnp.dot(hid, wd_v[:, 256 * p:256 * p + 256], preferred_element_type=F32)
        for b in range(8):
            dbuf[b % 2, b // 2, yy, zz] = jnp.concatenate(
                [part[8 * b:8 * b + 8, 0:128], part[8 * b:8 * b + 8, 128:256]], axis=0).astype(BF16)

    core_copy = rcopy(dbuf.at[1 - core], rcore, e_c.at[0], e_c.at[1], at_req(x * 2 + 1 - core))
    core_copy.start()
    core_copy.wait_recv()

    def fold_core(i):
        r1[i] = (dbuf[core, i].astype(F32) + rcore[i].astype(F32)).astype(BF16)

    loop(0, 4, fold_core)

    def ex_copy(o):
        xo = lax.rem(x + o, 4)
        return rcopy(r1.at[xo], rx.at[x], e_x.at[o], e_x.at[4 + x], at_req(xo * 2 + core))

    for o in (2, 1, 3):
        ex_copy(o).start()
    for o in range(1, 4):
        xo = lax.rem(x + o, 4)
        rcopy(r1.at[xo], rx.at[xo], e_x.at[o], e_x.at[4 + xo], me).wait_recv()
    xa, xb2, xc = lax.rem(x + 1, 4), lax.rem(x + 2, 4), lax.rem(x + 3, 4)

    def fold_x(i):
        r2[i] = (r1[x, i].astype(F32) + rx[xa, i].astype(F32)
                 + rx[xb2, i].astype(F32) + rx[xc, i].astype(F32)).astype(BF16)

    loop(0, 4, fold_x)

    def ey_copy(o):
        yo = lax.rem(y + o, 4)
        return rcopy(r2.at[yo], ry.at[y], e_y.at[o], e_y.at[4 + y], at_y(yo))

    for o in (2, 1, 3):
        ey_copy(o).start()
    for o in range(1, 4):
        yo = lax.rem(y + o, 4)
        rcopy(r2.at[yo], ry.at[yo], e_y.at[o], e_y.at[4 + yo], me).wait_recv()
    r3[...] = (r2[y].astype(F32) + ry[lax.rem(y + 1, 4)].astype(F32)
               + ry[lax.rem(y + 2, 4)].astype(F32) + ry[lax.rem(y + 3, 4)].astype(F32)).astype(BF16)

    def ez_copy(o):
        zo = lax.rem(z + o, 8)
        return rcopy(r3.at[zo], rz.at[z], e_z.at[o], e_z.at[8 + z], at_z(zo))

    loop(1, 8, lambda o: ez_copy(o).start())
    rz[z] = r3[z]

    def wait_ez(o):
        zo = lax.rem(z + o, 8)
        rcopy(r3.at[zo], rz.at[zo], e_z.at[o], e_z.at[8 + zo], me).wait_recv()

    loop(1, 8, wait_ez)
    own = xs[pl.ds(yz * 2, 2), pl.ds(pl.multiple_of(x * 16, 16), 16), :].astype(F32)
    own = jnp.where(core == 0, own[:, 0:8, :], own[:, 8:16, :])
    res = own.reshape(16, 128) + jnp.sum(rz[...].astype(F32), axis=0)
    out_ref[:, 0:128] = res[0:8, :].astype(BF16)
    out_ref[:, 128:256] = res[8:16, :].astype(BF16)

    def drain_attn(o):
        acc_copy(o).wait_send()
        stat_copy(o).wait_send()

    loop(1, 16, drain_attn)
    loop(1, 32, lambda o: p_copy(o).wait_send())

    def drain8(o):
        o_copy(o).wait_send()
        z_copy(o).wait_send()
        d_copy(o).wait_send()
        ez_copy(o).wait_send()

    loop(1, 8, drain8)
    for o in range(1, 4):
        y_copy(o).wait_send()
        x_copy(o).wait_send()
        ex_copy(o).wait_send()
        ey_copy(o).wait_send()
    for o in range(4):
        c_copy(o).wait_send()
    core_copy.wait_send()


def shards(query, cache_keys, cache_values, new_keys, new_values, lengths, residual_in, out_proj,
           norm_gain, adapter_down, tenant_adapter_up_matrix, tenant, w_gate, w_up, w_down):
    hbm = pl.BlockSpec(memory_space=pl.ANY)
    smem = pl.BlockSpec(memory_space=pltpu.SMEM)
    v = pltpu.VMEM
    dma = pltpu.SemaphoreType.DMA
    return pl.pallas_call(
        functools.partial(kernel, None),
        out_shape=jax.ShapeDtypeStruct((8, 256), BF16),
        in_specs=[hbm, hbm, hbm, hbm, hbm, smem, hbm, hbm, hbm, hbm, hbm, smem, hbm, hbm, hbm],
        out_specs=pl.BlockSpec(memory_space=pltpu.VMEM),
        scratch_shapes=[
            v((8, 8192), BF16), v((8, 128, 512), BF16), v((8, 128, 512), BF16), v((8, 512), BF16),
            v((8, 512), BF16), v((16, 128), BF16), v((512, 1024), BF16), v((64, 128), F32),
            v((1024, 256), BF16), v((256, 128), BF16), v((8192, 256), BF16), v((128, 8192), BF16),
            v((512, 128), F32), v((16, 32, 128), BF16), v((8, 128), F32), v((16, 32, 128), BF16),
            v((16, 8, 128), F32), v((128, 128), F32),
            v((8, 32, 128), BF16), v((4, 8, 16, 128), BF16), v((32, 16, 128), BF16), v((64, 64, 128), BF16),
            v((8, 128), F32), v((8, 8, 128), F32),
            v((2, 4, 4, 8, 16, 128), BF16), v((4, 4, 8, 16, 128), BF16), v((4, 4, 8, 16, 128), BF16),
            v((4, 4, 8, 16, 128), BF16), v((4, 8, 16, 128), BF16), v((4, 8, 16, 128), BF16),
            v((8, 16, 128), BF16), v((8, 16, 128), BF16),
            dma((13,)),
            dma((16,)), dma((16,)), dma((16,)), dma((16,)), dma((8,)), dma((8,)), dma((32,)), dma((32,)),
            dma((8,)), dma((8,)), dma((4,)), dma((4,)), dma((4,)), dma((4,)), dma((4,)), dma((4,)),
            dma((8,)), dma((8,)), dma((2,)), dma((8,)), dma((8,)), dma((16,)),
        ],
        compiler_params=pltpu.CompilerParams(
            collective_id=0, has_side_effects=True, vmem_limit_bytes=48 * 1024 * 1024),
    )(query, cache_keys, cache_values, new_keys, new_values, lengths, residual_in, out_proj,
      norm_gain.reshape(64, 128), adapter_down, tenant_adapter_up_matrix, tenant, w_gate, w_up, w_down)


def solution(mesh):
    placed = (
        P("req", "role"),
        P("req", "ctx", "role"),
        P("req", "ctx", "role"),
        P("req", "role"),
        P("req", "role"),
        P("req"),
        P(None, "req"),
        P(("role", "ctx"), "req"),
        P(),
        P("req", None),
        P(None, ("role", "req", "ctx")),
        P(),
        P(None, ("role", "req", "ctx")),
        P(None, ("role", "req", "ctx")),
        P(("role", "req", "ctx"), None),
    )
    return jax.shard_map(
        shards, mesh=mesh, in_specs=placed, out_specs=P("req", ("role", "ctx")), check_vma=False
    )
```

time: 653 us -> 85.7 us (0.13)
  the two profiles are of different devices: /device:TPU:1 before, /device:TPU:4 now
where the time goes in v1:
time: 85.7 us; the launch traced here: 85.2 us
  Pallas kernels  72.2 us (84%)
  local copies, waits for them, and re-layouts  13 us (15%)
    pallas_call x1, Pallas kernels, shards(): pl.pallas_call(functools.partial(kernel, None), out_shape=jax.ShapeDtypeS...  72.2 us
    unnamed x27, local copies, waits for them, and re-layouts  13 us

profile of v1, /device:TPU:4, one launch (start us, length us, event | category | flops | bytes accessed | tf_op | source)
XLA Modules:
  0.0 85.2 jit_solution(4205372501958729165)
XLA Ops:
  0.0 0.0 copy-start
  0.0 1.6 %copy-done = bf16[8192,128]{1,0:T(8,128)(2,1)S(1)} copy-done((bf16[8192,128]{1,0:T(8,128)(2,1)S(1)}, bf16[8192,128]{1,0:T(8,128)(2,1)}, u32[]{:S(2)}) %copy-start) | copy-done | bytes 2097176
  1.6 0.0 copy-start.1
  1.6 1.2 %copy-done.1 = bf16[8,128,512]{2,1,0:T(8,128)(2,1)S(1)} copy-done((bf16[8,128,512]{2,1,0:T(8,128)(2,1)S(1)}, bf16[8,128,512]{2,1,0:T(8,128)(2,1)}, u32[]{:S(2)}) %copy-start.1) | copy-done | bytes 1048600
  2.8 0.0 copy-start.2
  2.8 1.2 %copy-done.2 = bf16[8,128,512]{2,1,0:T(8,128)(2,1)S(1)} copy-done((bf16[8,128,512]{2,1,0:T(8,128)(2,1)S(1)}, bf16[8,128,512]{2,1,0:T(8,128)(2,1)}, u32[]{:S(2)}) %copy-start.2) | copy-done | bytes 1048600
  4.0 0.0 copy-start.3
  4.0 1.2 %copy-done.3 = bf16[512,1024]{1,0:T(8,128)(2,1)S(1)} copy-done((bf16[512,1024]{1,0:T(8,128)(2,1)S(1)}, bf16[512,1024]{1,0:T(8,128)(2,1)}, u32[]{:S(2)}) %copy-start.3) | copy-done | bytes 1048600
  5.3 0.0 copy-start.4
  5.3 1.0 %copy-done.4 = bf16[1024,256]{1,0:T(8,128)(2,1)S(1)} copy-done((bf16[1024,256]{1,0:T(8,128)(2,1)S(1)}, bf16[1024,256]{1,0:T(8,128)(2,1)}, u32[]{:S(2)}) %copy-start.4) | copy-done | bytes 524312
  6.3 0.0 copy-start.5
  6.3 0.9 %copy-done.5 = bf16[8,8192]{1,0:T(8,128)(2,1)S(1)} copy-done((bf16[8,8192]{1,0:T(8,128)(2,1)S(1)}, bf16[8,8192]{1,0:T(8,128)(2,1)}, u32[]{:S(2)}) %copy-start.5) | copy-done | bytes 131096
  7.2 0.0 copy-start.6
  7.2 0.9 %copy-done.6 = bf16[64,1024]{1,0:T(8,128)(2,1)S(1)} copy-done((bf16[64,1024]{1,0:T(8,128)(2,1)S(1)}, bf16[64,1024]{1,0:T(8,128)(2,1)}, u32[]{:S(2)}) %copy-start.6) | copy-done | bytes 131096
  8.1 0.8 copy-done.7
  9.0 0.8 copy-done.8
  9.7 0.0 copy-start.9
  9.7 0.7 copy-done.9
  10.4 0.0 copy-start.10
  10.4 0.7 copy-done.10
  11.1 0.7 copy-done.11
  11.8 0.7 copy-done.12
  12.4 72.2 %shard_map.145 = bf16[8,256]{1,0:T(8,128)(2,1)S(1)} custom-call(bf16[8,8192]{1,0:T(8,128)(2,1)S(1)} %copy-done.5, bf16[8,128,512]{2,1,0:T(8,128)(2,1)S(1)} %copy-done.1, bf16[8,128,512]{2,1,0:T(8,128)(2,1)S(1)} %copy-done.2, bf16[8,512]{1,0:T(8,128)(2,1)S(1)} %copy-done.9, bf16[8,512]{1,0:T(8,128)(2,1)S(1)} %copy-done.10, s32[8]{0:T(128)S(1)} %copy-done.11, ...), custom_call_target="tpu_custom_call" | custom-call | tf_op jit(solution)/shard_map/pallas_call | solution.py:429
  84.6 0.6 copy.17
  (4 shorter events, 0.0 us)
Async XLA Ops:
  0.0 1.6 %copy-start = (bf16[8192,128]{1,0:T(8,128)(2,1)S(1)}, bf16[8192,128]{1,0:T(8,128)(2,1)}, u32[]{:S(2)}) copy-start(bf16[8192,128]{1,0:T(8,128)(2,1)} %wg_h.1) | copy-start | bytes 6291460
  1.6 1.2 %copy-start.1 = (bf16[8,128,512]{2,1,0:T(8,128)(2,1)S(1)}, bf16[8,128,512]{2,1,0:T(8,128)(2,1)}, u32[]{:S(2)}) copy-start(bf16[8,128,512]{2,1,0:T(8,128)(2,1)} %ck_h.1) | copy-start | bytes 3145732
  2.8 1.2 %copy-start.2 = (bf16[8,128,512]{2,1,0:T(8,128)(2,1)S(1)}, bf16[8,128,512]{2,1,0:T(8,128)(2,1)}, u32[]{:S(2)}) copy-start(bf16[8,128,512]{2,1,0:T(8,128)(2,1)} %cv_h.1) | copy-start | bytes 3145732
  4.0 1.2 %copy-start.3 = (bf16[512,1024]{1,0:T(8,128)(2,1)S(1)}, bf16[512,1024]{1,0:T(8,128)(2,1)}, u32[]{:S(2)}) copy-start(bf16[512,1024]{1,0:T(8,128)(2,1)} %wo_h.1) | copy-start | bytes 3145732
  5.3 1.0 %copy-start.4 = (bf16[1024,256]{1,0:T(8,128)(2,1)S(1)}, bf16[1024,256]{1,0:T(8,128)(2,1)}, u32[]{:S(2)}) copy-start(bf16[1024,256]{1,0:T(8,128)(2,1)} %ad_h.1) | copy-start | bytes 1572868
  6.3 0.9 %copy-start.5 = (bf16[8,8192]{1,0:T(8,128)(2,1)S(1)}, bf16[8,8192]{1,0:T(8,128)(2,1)}, u32[]{:S(2)}) copy-start(bf16[8,8192]{1,0:T(8,128)(2,1)} %q_h.1) | copy-start | bytes 393220
  7.2 0.9 %copy-start.6 = (bf16[64,1024]{1,0:T(8,128)(2,1)S(1)}, bf16[64,1024]{1,0:T(8,128)(2,1)}, u32[]{:S(2)}) copy-start(bf16[64,1024]{1,0:T(8,128)(2,1)} %res_h.1) | copy-start | bytes 393220
  8.1 0.8 copy-start.7
  9.0 0.8 copy-start.8
  9.7 0.7 copy-start.9
  10.4 0.7 copy-start.10
  11.1 0.7 copy-start.11
  11.8 0.7 copy-start.12

commit v2 on v1

--- a/solution.py
+++ b/solution.py
@@ -15,6 +15,12 @@
 EPS = 1e-05
 LOW = -1e30
 NT = (((1,), (1,)), ((), ()))
+Z_FAR = (4, 3, 5, 2, 6, 1, 7)
+XY_FAR = ((2, 2), (1, 2), (3, 2), (2, 1), (2, 3), (1, 1), (1, 3), (3, 1), (3, 3),
+          (2, 0), (0, 2), (1, 0), (3, 0), (0, 1), (0, 3))
+YZ_FAR = tuple((dy, dz) for dz in Z_FAR + (0,) for dy in (2, 1, 3, 0) if dy or dz)
+REQ_FAR = ((2, 1), (2, 0), (1, 1), (3, 1), (1, 0), (3, 0), (0, 1))
+CTX_FAR = tuple((dh, dz) for dz in Z_FAR + (0,) for dh in (1, 0) if dh or dz)
 
 
 def rcopy(src, dst, ssem, rsem, dev):
@@ -37,9 +43,9 @@
     out_ref,
     q_v, ck_v, cv_v, nk_v, nv_v, res_v, wo_v, gain_v, ad_v, tu_v, wgu_v, wd_v,
     qrows, acc_s, stat_s, racc, rstat, rt_v,
-    ogath, psend, rpart, xs, ad_s, rad, dbuf, rcore, r1, rx, r2, ry, r3, rz,
+    ogath, psend, rpart, xs, ad_s, rad, dbuf, rcore, r1, rx, r3, rz,
     lsem,
-    sa_s, sa_r, ss_s, ss_r, so_s, so_r, sp_s, sp_r, sz_s, sz_r, sy_s, sy_r, sx_s, sx_r, sc_s, sc_r,
+    sa_s, sa_r, ss_s, ss_r, so_s, so_r, sp_s, sp_r, sz_s, sz_r, sx_s, sx_r, sc_s, sc_r,
     sd_s, sd_r, e_c, e_x, e_y, e_z,
 ):
     role = lax.axis_index("role")
@@ -59,11 +65,17 @@
     def at_req(i):
         return (role, i, ctx)
 
-    def at_y(i):
-        return (lax.rem(i, 2), req, lax.div(i, 2) * 8 + z)
+    def at_xy(xo, yo):
+        return (lax.rem(yo, 2), xo * 2 + core, lax.div(yo, 2) * 8 + z)
 
     def at_z(i):
         return (role, req, yhi * 8 + i)
+
+    drains = []
+
+    def finish():
+        for d in drains:
+            d()
 
     local = [
         pltpu.make_async_copy(q_h, q_v, lsem.at[0]),
@@ -103,7 +115,7 @@
     stat_lane = lax.broadcasted_iota(jnp.int32, (128, 128), 1)
     local[0].wait()
     local[1].wait()
-    local[2].wait()
+    probs = []
     stat = jnp.zeros((128, 128), F32)
     for k in range(4):
         qk = jnp.concatenate(
@@ -119,32 +131,43 @@
         w = jnp.where(usable, jnp.exp(sc - top), 0.0)
         wb = w.astype(BF16).astype(F32)
         tot = jnp.sum(wb, axis=-1, keepdims=True)
+        probs.append(wb)
+        stat = jnp.where(stat_lane == 2 * k, top.reshape(128, 1), stat)
+        stat = jnp.where(stat_lane == 2 * k + 1, tot.reshape(128, 1), stat)
+    stat_s[...] = stat.T[0:8, :]
+
+    pl.semaphore_wait(barrier, 38)
+
+    def ctx_peer(dh, dz):
+        return lax.rem(yhi + dh, 2) * 8 + lax.rem(z + dz, 8)
+
+    def stat_copy(dh, dz):
+        return rcopy(stat_s, rstat.at[ctx], ss_s.at[dh * 8 + dz], ss_r.at[ctx], (role, req, ctx_peer(dh, dz)))
+
+    def acc_copy(dh, dz):
+        c = ctx_peer(dh, dz)
+        return rcopy(acc_s.at[c], racc.at[ctx], sa_s.at[dh * 8 + dz], sa_r.at[ctx], (role, req, c))
+
+    for o in CTX_FAR:
+        stat_copy(*o).start()
+    rstat[ctx] = stat_s[...]
+    local[2].wait()
+    for k in range(4):
         big = jnp.concatenate(
-            [jnp.where(rowmod == r, wb, 0.0).reshape(128, 128).astype(BF16) for r in range(8)], axis=1)
+            [jnp.where(rowmod == r, probs[k], 0.0).reshape(128, 128).astype(BF16) for r in range(8)], axis=1)
         vk = cv_v[:, :, k * 128:(k + 1) * 128].reshape(1024, 128)
         acc = jnp.dot(big, vk, preferred_element_type=F32)
         acc_s[4 * k:4 * k + 4] = acc.astype(BF16).reshape(4, 32, 128)
-        stat = jnp.where(stat_lane == 2 * k, top.reshape(128, 1), stat)
-        stat = jnp.where(stat_lane == 2 * k + 1, tot.reshape(128, 1), stat)
-    stat_s[...] = stat.T[0:8, :]
-
-    pl.semaphore_wait(barrier, 38)
-
-    def acc_copy(o):
-        c = lax.rem(ctx + o, 16)
-        return rcopy(acc_s.at[c], racc.at[ctx], sa_s.at[o], sa_r.at[ctx], (role, req, c))
-
-    def stat_copy(o):
-        c = lax.rem(ctx + o, 16)
-        return rcopy(stat_s, rstat.at[ctx], ss_s.at[o], ss_r.at[ctx], (role, req, c))
-
-    def send_attn(o):
-        acc_copy(o).start()
-        stat_copy(o).start()
-
-    loop(1, 16, send_attn)
+    for o in CTX_FAR:
+        acc_copy(*o).start()
     racc[ctx] = acc_s[ctx]
-    rstat[ctx] = stat_s[...]
+
+    def drain_attn():
+        for o in CTX_FAR:
+            acc_copy(*o).wait_send()
+            stat_copy(*o).wait_send()
+
+    drains.append(drain_attn)
 
     kh = lax.div(ctx, 4)
     local[3].wait()
@@ -156,12 +179,15 @@
     s_self = (jnp.sum(q32 * nk[None], axis=-1, keepdims=True) * factor).reshape(32, 1)
     nv32 = jnp.broadcast_to(nv[None], (4, 8, 128)).reshape(32, 128)
 
-    def wait_attn(o):
+    def wait_stat(o):
+        c = lax.rem(ctx + o, 16)
+        rcopy(stat_s, rstat.at[c], ss_s.at[o], ss_r.at[c], me).wait_recv()
+
+    def wait_acc(o):
         c = lax.rem(ctx + o, 16)
         rcopy(acc_s.at[c], racc.at[c], sa_s.at[o], sa_r.at[c], me).wait_recv()
-        rcopy(stat_s, rstat.at[c], ss_s.at[o], ss_r.at[c], me).wait_recv()
-
-    loop(1, 16, wait_attn)
+
+    loop(1, 16, wait_stat)
     rt_v[...] = rstat[...].reshape(128, 128).T
     st = rt_v[pl.ds(pl.multiple_of(lax.rem(ctx, 4) * 32, 32), 32), :]
     st = pltpu.roll(st, lax.rem(128 - 2 * kh, 128), 1)
@@ -172,15 +198,20 @@
     wgt = jnp.where(first, jnp.exp(tops - high), 0.0)
     w_self = jnp.exp(s_self - high)
     den = jnp.sum(wgt * pltpu.roll(st, 127, 1), axis=-1, keepdims=True) + w_self
-    o_acc = w_self * nv32
+    wgt = wgt / den
+    o_acc = (w_self / den) * nv32
+    loop(1, 16, wait_acc)
     for s in range(16):
         o_acc = o_acc + wgt[:, 8 * s:8 * s + 1] * racc[s].astype(F32)
-    ogath[req] = (o_acc / den).astype(BF16)
-
-    def o_copy(o):
-        return rcopy(ogath.at[req], ogath.at[req], so_s.at[o], so_r.at[req], at_req(lax.rem(req + o, 8)))
-
-    loop(1, 8, lambda o: o_copy(o).start())
+    ogath[req] = o_acc.astype(BF16)
+
+    def o_copy(dx, dc):
+        peer = at_req(lax.rem(x + dx, 4) * 2 + lax.rem(core + dc, 2))
+        return rcopy(ogath.at[req], ogath.at[req], so_s.at[dx * 2 + dc], so_r.at[req], peer)
+
+    for o in REQ_FAR:
+        o_copy(*o).start()
+        drains.append(lambda o=o: o_copy(*o).wait_send())
 
     def wait_o(o):
         c = lax.rem(req + o, 8)
@@ -196,13 +227,19 @@
         for zz in range(8):
             psend[yy, zz] = proj[16 * yy:16 * yy + 16, 128 * zz:128 * zz + 128].astype(BF16)
 
-    def p_copy(o):
-        d = lax.rem(yz + o, 32)
-        rr, cc = lax.div(d, 16), lax.rem(d, 16)
-        return rcopy(psend.at[lax.div(cc, 8) * 2 + rr, lax.rem(cc, 8)], rpart.at[yz],
-                     sp_s.at[o], sp_r.at[yz], (rr, req, cc))
-
-    loop(1, 32, lambda o: p_copy(o).start())
+    def p_copy(dy, dz):
+        yo, zo = lax.rem(y + dy, 4), lax.rem(z + dz, 8)
+        return rcopy(psend.at[yo, zo], rpart.at[yz], sp_s.at[dy * 8 + dz], sp_r.at[yz],
+                     (lax.rem(yo, 2), req, lax.div(yo, 2) * 8 + zo))
+
+    for o in YZ_FAR:
+        p_copy(*o).start()
+
+    def drain_p():
+        for o in YZ_FAR:
+            p_copy(*o).wait_send()
+
+    drains.append(drain_p)
     rpart[yz] = psend[y, z]
 
     def wait_p(o):
@@ -221,7 +258,9 @@
     def z_copy(o):
         return rcopy(z_ref(z), z_ref(z), sz_s.at[o], sz_r.at[z], at_z(lax.rem(z + o, 8)))
 
-    loop(1, 8, lambda o: z_copy(o).start())
+    for o in Z_FAR:
+        z_copy(o).start()
+        drains.append(lambda o=o: z_copy(o).wait_send())
 
     def wait_z(o):
         c = lax.rem(z + o, 8)
@@ -229,31 +268,33 @@
 
     loop(1, 8, wait_z)
 
-    def y_ref(i):
-        return xs.at[pl.ds(req * 8, 8), pl.ds(pl.multiple_of(i * 16, 16), 16)]
-
-    def y_copy(o):
-        return rcopy(y_ref(y), y_ref(y), sy_s.at[o], sy_r.at[y], at_y(lax.rem(y + o, 4)))
-
-    for o in range(1, 4):
-        y_copy(o).start()
-    for o in range(1, 4):
-        c = lax.rem(y + o, 4)
-        rcopy(y_ref(c), y_ref(c), sy_s.at[o], sy_r.at[c], me).wait_recv()
+    def y_ref(b, yo):
+        return xs.at[pl.ds(b * 8, 8), pl.ds(pl.multiple_of(yo * 16, 16), 16)]
+
+    def xy_copy(dx, dy):
+        return rcopy(y_ref(req, y), y_ref(req, y), sx_s.at[dx, dy], sx_r.at[x, y],
+                     at_xy(lax.rem(x + dx, 4), lax.rem(y + dy, 4)))
+
+    def xy_wait(dx, dy):
+        xo, yo = lax.rem(x + dx, 4), lax.rem(y + dy, 4)
+        ref = y_ref(xo * 2 + core, yo)
+        rcopy(ref, ref, sx_s.at[dx, dy], sx_r.at[xo, yo], me).wait_recv()
+
+    for o in XY_FAR:
+        xy_copy(*o).start()
+        drains.append(lambda o=o: xy_copy(*o).wait_send())
 
     def b_ref(b):
         return xs.at[pl.ds(b * 8, 8)]
-
-    def x_copy(o):
-        return rcopy(b_ref(req), b_ref(req), sx_s.at[o], sx_r.at[x], at_req(lax.rem(x + o, 4) * 2 + core))
 
     def c_copy(o):
         b = lax.rem(x + o, 4) * 2 + core
         return rcopy(b_ref(b), b_ref(b), sc_s.at[o], sc_r.at[lax.rem(x + o, 4)], at_req(x * 2 + 1 - core))
 
-    for o in (1, 3, 2):
-        x_copy(o).start()
+    for dy in (1, 3, 2):
+        xy_wait(0, dy)
     c_copy(0).start()
+    drains.append(lambda: c_copy(0).wait_send())
     local[7].wait()
     local[8].wait()
     local[10].wait()
@@ -288,18 +329,23 @@
         packed = jnp.where(owner == i, v, packed)
     ad_s[...] = packed
 
-    def d_copy(o):
-        return rcopy(ad_s, rad.at[req], sd_s.at[o], sd_r.at[req], at_req(lax.rem(req + o, 8)))
-
-    loop(1, 8, lambda o: d_copy(o).start())
+    def d_copy(dx, dc):
+        peer = at_req(lax.rem(x + dx, 4) * 2 + lax.rem(core + dc, 2))
+        return rcopy(ad_s, rad.at[req], sd_s.at[dx * 2 + dc], sd_r.at[req], peer)
+
+    for o in REQ_FAR:
+        d_copy(*o).start()
+        drains.append(lambda o=o: d_copy(*o).wait_send())
     rad[req] = packed
     gu = gate_up(req, xg)
     for o in (0, 1, 3, 2):
         xo = lax.rem(x + o, 4)
         if o > 0:
             b = xo * 2 + core
-            rcopy(b_ref(b), b_ref(b), sx_s.at[o], sx_r.at[xo], me).wait_recv()
+            for dy in (0, 1, 3, 2):
+                xy_wait(o, dy)
             c_copy(o).start()
+            drains.append(lambda o=o: c_copy(o).wait_send())
             s1, xg = block(b)
             sq = sq + s1
             gu = gu + gate_up(b, xg)
@@ -342,6 +388,7 @@
 
     core_copy = rcopy(dbuf.at[1 - core], rcore, e_c.at[0], e_c.at[1], at_req(x * 2 + 1 - core))
     core_copy.start()
+    drains.append(core_copy.wait_send)
     core_copy.wait_recv()
 
     def fold_core(i):
@@ -349,40 +396,37 @@
 
     loop(0, 4, fold_core)
 
-    def ex_copy(o):
-        xo = lax.rem(x + o, 4)
-        return rcopy(r1.at[xo], rx.at[x], e_x.at[o], e_x.at[4 + x], at_req(xo * 2 + core))
-
-    for o in (2, 1, 3):
-        ex_copy(o).start()
-    for o in range(1, 4):
-        xo = lax.rem(x + o, 4)
-        rcopy(r1.at[xo], rx.at[xo], e_x.at[o], e_x.at[4 + xo], me).wait_recv()
-    xa, xb2, xc = lax.rem(x + 1, 4), lax.rem(x + 2, 4), lax.rem(x + 3, 4)
-
-    def fold_x(i):
-        r2[i] = (r1[x, i].astype(F32) + rx[xa, i].astype(F32)
-                 + rx[xb2, i].astype(F32) + rx[xc, i].astype(F32)).astype(BF16)
-
-    loop(0, 4, fold_x)
-
-    def ey_copy(o):
-        yo = lax.rem(y + o, 4)
-        return rcopy(r2.at[yo], ry.at[y], e_y.at[o], e_y.at[4 + y], at_y(yo))
-
-    for o in (2, 1, 3):
-        ey_copy(o).start()
-    for o in range(1, 4):
-        yo = lax.rem(y + o, 4)
-        rcopy(r2.at[yo], ry.at[yo], e_y.at[o], e_y.at[4 + yo], me).wait_recv()
-    r3[...] = (r2[y].astype(F32) + ry[lax.rem(y + 1, 4)].astype(F32)
-               + ry[lax.rem(y + 2, 4)].astype(F32) + ry[lax.rem(y + 3, 4)].astype(F32)).astype(BF16)
+    def ex_copy(dx, dy):
+        xo, yo = lax.rem(x + dx, 4), lax.rem(y + dy, 4)
+        return rcopy(r1.at[xo, yo], rx.at[x, y], e_x.at[dx, dy], e_y.at[x, y], at_xy(xo, yo))
+
+    for o in XY_FAR:
+        ex_copy(*o).start()
+        drains.append(lambda o=o: ex_copy(*o).wait_send())
+    rx[x, y] = r1[x, y]
+
+    def wait_ex(o):
+        i = lax.rem(x * 4 + y + o, 16)
+        xo, yo = lax.div(i, 4), lax.rem(i, 4)
+        rcopy(r1.at[xo, yo], rx.at[xo, yo], e_x.at[xo, yo], e_y.at[xo, yo], me).wait_recv()
+
+    loop(1, 16, wait_ex)
+
+    def fold_xy(i):
+        part = rx[0, 0, i].astype(F32)
+        for j in range(1, 16):
+            part = part + rx[j // 4, j % 4, i].astype(F32)
+        r3[i] = part.astype(BF16)
+
+    loop(0, 8, fold_xy)
 
     def ez_copy(o):
         zo = lax.rem(z + o, 8)
         return rcopy(r3.at[zo], rz.at[z], e_z.at[o], e_z.at[8 + z], at_z(zo))
 
-    loop(1, 8, lambda o: ez_copy(o).start())
+    for o in Z_FAR:
+        ez_copy(o).start()
+        drains.append(lambda o=o: ez_copy(o).wait_send())
     rz[z] = r3[z]
 
     def wait_ez(o):
@@ -395,29 +439,7 @@
     res = own.reshape(16, 128) + jnp.sum(rz[...].astype(F32), axis=0)
     out_ref[:, 0:128] = res[0:8, :].astype(BF16)
     out_ref[:, 128:256] = res[8:16, :].astype(BF16)
-
-    def drain_attn(o):
-        acc_copy(o).wait_send()
-        stat_copy(o).wait_send()
-
-    loop(1, 16, drain_attn)
-    loop(1, 32, lambda o: p_copy(o).wait_send())
-
-    def drain8(o):
-        o_copy(o).wait_send()
-        z_copy(o).wait_send()
-        d_copy(o).wait_send()
-        ez_copy(o).wait_send()
-
-    loop(1, 8, drain8)
-    for o in range(1, 4):
-        y_copy(o).wait_send()
-        x_copy(o).wait_send()
-        ex_copy(o).wait_send()
-        ey_copy(o).wait_send()
-    for o in range(4):
-        c_copy(o).wait_send()
-    core_copy.wait_send()
+    finish()
 
 
 def shards(query, cache_keys, cache_values, new_keys, new_values, lengths, residual_in, out_proj,
@@ -440,15 +462,14 @@
             v((8, 32, 128), BF16), v((4, 8, 16, 128), BF16), v((32, 16, 128), BF16), v((64, 64, 128), BF16),
             v((8, 128), F32), v((8, 8, 128), F32),
             v((2, 4, 4, 8, 16, 128), BF16), v((4, 4, 8, 16, 128), BF16), v((4, 4, 8, 16, 128), BF16),
-            v((4, 4, 8, 16, 128), BF16), v((4, 8, 16, 128), BF16), v((4, 8, 16, 128), BF16),
-            v((8, 16, 128), BF16), v((8, 16, 128), BF16),
+            v((4, 4, 8, 16, 128), BF16), v((8, 16, 128), BF16), v((8, 16, 128), BF16),
             dma((13,)),
             dma((16,)), dma((16,)), dma((16,)), dma((16,)), dma((8,)), dma((8,)), dma((32,)), dma((32,)),
-            dma((8,)), dma((8,)), dma((4,)), dma((4,)), dma((4,)), dma((4,)), dma((4,)), dma((4,)),
-            dma((8,)), dma((8,)), dma((2,)), dma((8,)), dma((8,)), dma((16,)),
+            dma((8,)), dma((8,)), dma((4, 4)), dma((4, 4)), dma((4,)), dma((4,)),
+            dma((8,)), dma((8,)), dma((2,)), dma((4, 4)), dma((4, 4)), dma((16,)),
         ],
         compiler_params=pltpu.CompilerParams(
-            collective_id=0, has_side_effects=True, vmem_limit_bytes=48 * 1024 * 1024),
+            collective_id=0, has_side_effects=True, vmem_limit_bytes=60 * 1024 * 1024),
     )(query, cache_keys, cache_values, new_keys, new_values, lengths, residual_in, out_proj,
       norm_gain.reshape(64, 128), adapter_down, tenant_adapter_up_matrix, tenant, w_gate, w_up, w_down)
 

time: 85.7 us -> 65.2 us (0.76)
  the two profiles are of different devices: /device:TPU:4 before, /device:TPU:1 now
where the time goes in v2:
time: 65.2 us; the launch traced here: 65.1 us
  Pallas kernels  63.8 us (98%)
  local copies, waits for them, and re-layouts  1.28 us (2%)
    pallas_call x1, Pallas kernels, shards(): pl.pallas_call(functools.partial(kernel, None), out_shape=jax.ShapeDtypeS...  63.8 us

profile of v2, /device:TPU:1, one launch (start us, length us, event | category | flops | bytes accessed | tf_op | source)
XLA Modules:
  0.0 65.1 jit_solution(5307533480892416715)
XLA Ops:
  0.0 63.8 %shard_map.145 = bf16[8,256]{1,0:T(8,128)(2,1)} custom-call(bf16[8,8192]{1,0:T(8,128)(2,1)} %q_h.1, bf16[8,128,512]{2,1,0:T(8,128)(2,1)} %ck_h.1, bf16[8,128,512]{2,1,0:T(8,128)(2,1)} %cv_h.1, bf16[8,512]{1,0:T(8,128)(2,1)} %nk_h.1, bf16[8,512]{1,0:T(8,128)(2,1)} %nv_h.1, s32[8]{0:T(128)} %len_s.1, bf16[64,1024]{1,0:T(8,128)(2,1)} %res_h.1, ...), custom_call_target="tpu_custom_call" | custom-call | tf_op jit(solution)/shard_map/pallas_call | solution.py:451
  63.8 1.3 %copy.17 = bf16[8,256]{1,0:T(8,128)(2,1)} copy(bf16[8,256]{1,0:T(8,128)(2,1)} %shard_map.145) | data formatting | bytes 8192

commit v3 on v2

--- a/solution.py
+++ b/solution.py
@@ -19,8 +19,8 @@
 XY_FAR = ((2, 2), (1, 2), (3, 2), (2, 1), (2, 3), (1, 1), (1, 3), (3, 1), (3, 3),
           (2, 0), (0, 2), (1, 0), (3, 0), (0, 1), (0, 3))
 YZ_FAR = tuple((dy, dz) for dz in Z_FAR + (0,) for dy in (2, 1, 3, 0) if dy or dz)
+HALF_FAR = tuple((dx, dc, dh) for dh in (1, 0) for dx in (2, 1, 3, 0) for dc in (1, 0) if dx or dc or dh)
 REQ_FAR = ((2, 1), (2, 0), (1, 1), (3, 1), (1, 0), (3, 0), (0, 1))
-CTX_FAR = tuple((dh, dz) for dz in Z_FAR + (0,) for dh in (1, 0) if dh or dz)
 
 
 def rcopy(src, dst, ssem, rsem, dev):
@@ -42,10 +42,10 @@
     q_h, ck_h, cv_h, nk_h, nv_h, len_s, res_h, wo_h, gain_h, ad_h, tu_h, ten_s, wg_h, wu_h, wd_h,
     out_ref,
     q_v, ck_v, cv_v, nk_v, nv_v, res_v, wo_v, gain_v, ad_v, tu_v, wgu_v, wd_v,
-    qrows, acc_s, stat_s, racc, rstat, rt_v,
+    acc_s, stat_s, racc, rstat, rt_v, lse_s, oh_s, rl,
     ogath, psend, rpart, xs, ad_s, rad, dbuf, rcore, r1, rx, r3, rz,
     lsem,
-    sa_s, sa_r, ss_s, ss_r, so_s, so_r, sp_s, sp_r, sz_s, sz_r, sx_s, sx_r, sc_s, sc_r,
+    go, sa_s, sa_r, ss_s, ss_r, sl_s, sl_r, so_s, so_r, sp_s, sp_r, sz_s, sz_r, sx_s, sx_r, sc_s, sc_r,
     sd_s, sd_r, e_c, e_x, e_y, e_z,
 ):
     role = lax.axis_index("role")
@@ -59,14 +59,14 @@
     yz = role * 16 + ctx
     me = (role, req, ctx)
 
-    def at_yz(i):
-        return (lax.div(i, 16), req, lax.rem(i, 16))
-
     def at_req(i):
         return (role, i, ctx)
 
     def at_xy(xo, yo):
         return (lax.rem(yo, 2), xo * 2 + core, lax.div(yo, 2) * 8 + z)
+
+    def at_y(i):
+        return (lax.rem(i, 2), req, lax.div(i, 2) * 8 + z)
 
     def at_z(i):
         return (role, req, yhi * 8 + i)
@@ -95,14 +95,20 @@
         pltpu.make_async_copy(wu_h, wgu_v.at[:, pl.ds(128, 128)], lsem.at[11]),
         pltpu.make_async_copy(wd_h, wd_v, lsem.at[12]),
     ]
-    for c in local:
-        c.start()
+    for i in (0, 1, 3, 2, 4, 5, 6, 7, 8, 9, 10, 11, 12):
+        local[i].start()
 
     barrier = pltpu.get_barrier_semaphore()
-    loop(1, 32, lambda o: pl.semaphore_signal(
-        barrier, inc=1, device_id=at_yz(lax.rem(yz + o, 32)), device_id_type=MESH))
-    loop(1, 8, lambda o: pl.semaphore_signal(
-        barrier, inc=1, device_id=at_req(lax.rem(req + o, 8)), device_id_type=MESH))
+
+    def greet(dev):
+        pl.semaphore_signal(barrier, inc=1, device_id=dev, device_id_type=MESH)
+
+    for o in Z_FAR:
+        greet(at_z(lax.rem(z + o, 8)))
+    for dx, dc in REQ_FAR:
+        greet(at_req(lax.rem(x + dx, 4) * 2 + lax.rem(core + dc, 2)))
+    for o in (2, 1, 3):
+        greet(at_y(lax.rem(y + o, 4)))
 
     factor = 1.0 / math.sqrt(HD)
     sub = lax.broadcasted_iota(jnp.int32, (8, 128), 0)
@@ -115,113 +121,142 @@
     stat_lane = lax.broadcasted_iota(jnp.int32, (128, 128), 1)
     local[0].wait()
     local[1].wait()
+    local[3].wait()
     probs = []
+    fresh = []
     stat = jnp.zeros((128, 128), F32)
     for k in range(4):
         qk = jnp.concatenate(
             [q_v[:, (k * 16 + g) * 128:(k * 16 + g + 1) * 128].astype(F32) for g in range(16)], axis=0)
-        qrows[k * 128:(k + 1) * 128, :] = qk
+        nk = nk_v[:, k * 128:(k + 1) * 128].astype(F32)
+        own = jnp.sum(qk.reshape(16, 8, 128) * nk[None], axis=-1, keepdims=True) * factor
+        own = jnp.where(ctx == 0, own, LOW)
         kk = ck_v[:, :, k * 128:(k + 1) * 128].reshape(1024, 128)
         full = lax.dot_general(qk.astype(BF16), kk, NT, preferred_element_type=F32)
         sc = jnp.zeros((16, 8, 128), F32)
         for r in range(8):
             sc = jnp.where(rowmod == r, full[:, r * 128:(r + 1) * 128].reshape(16, 8, 128), sc)
         sc = jnp.where(usable, sc * factor, LOW)
-        top = jnp.max(sc, axis=-1, keepdims=True)
+        top = jnp.maximum(jnp.max(sc, axis=-1, keepdims=True), own)
         w = jnp.where(usable, jnp.exp(sc - top), 0.0)
         wb = w.astype(BF16).astype(F32)
-        tot = jnp.sum(wb, axis=-1, keepdims=True)
+        w_own = jnp.where(ctx == 0, jnp.exp(own - top), 0.0)
+        tot = jnp.sum(wb, axis=-1, keepdims=True) + w_own
         probs.append(wb)
+        fresh.append(w_own)
         stat = jnp.where(stat_lane == 2 * k, top.reshape(128, 1), stat)
         stat = jnp.where(stat_lane == 2 * k + 1, tot.reshape(128, 1), stat)
     stat_s[...] = stat.T[0:8, :]
 
-    pl.semaphore_wait(barrier, 38)
-
-    def ctx_peer(dh, dz):
-        return lax.rem(yhi + dh, 2) * 8 + lax.rem(z + dz, 8)
-
-    def stat_copy(dh, dz):
-        return rcopy(stat_s, rstat.at[ctx], ss_s.at[dh * 8 + dz], ss_r.at[ctx], (role, req, ctx_peer(dh, dz)))
-
-    def acc_copy(dh, dz):
-        c = ctx_peer(dh, dz)
-        return rcopy(acc_s.at[c], racc.at[ctx], sa_s.at[dh * 8 + dz], sa_r.at[ctx], (role, req, c))
-
-    for o in CTX_FAR:
-        stat_copy(*o).start()
-    rstat[ctx] = stat_s[...]
+    pl.semaphore_wait(barrier, 17)
+    for o in (2, 1, 3):
+        pl.semaphore_signal(go, inc=1, device_id=at_y(lax.rem(y + o, 4)), device_id_type=MESH)
+
+    def stat_copy(o):
+        return rcopy(stat_s, rstat.at[z], ss_s.at[o], ss_r.at[z], at_z(lax.rem(z + o, 8)))
+
+    def acc_copy(o):
+        zo = lax.rem(z + o, 8)
+        return rcopy(acc_s.at[:, zo], racc.at[z], sa_s.at[o], sa_r.at[z], at_z(zo))
+
+    for o in Z_FAR:
+        stat_copy(o).start()
+        drains.append(lambda o=o: stat_copy(o).wait_send())
+    rstat[z] = stat_s[...]
     local[2].wait()
+    local[4].wait()
     for k in range(4):
         big = jnp.concatenate(
             [jnp.where(rowmod == r, probs[k], 0.0).reshape(128, 128).astype(BF16) for r in range(8)], axis=1)
         vk = cv_v[:, :, k * 128:(k + 1) * 128].reshape(1024, 128)
-        acc = jnp.dot(big, vk, preferred_element_type=F32)
-        acc_s[4 * k:4 * k + 4] = acc.astype(BF16).reshape(4, 32, 128)
-    for o in CTX_FAR:
-        acc_copy(*o).start()
-    racc[ctx] = acc_s[ctx]
-
-    def drain_attn():
-        for o in CTX_FAR:
-            acc_copy(*o).wait_send()
-            stat_copy(*o).wait_send()
-
-    drains.append(drain_attn)
-
-    kh = lax.div(ctx, 4)
-    local[3].wait()
-    local[4].wait()
-    col = pl.ds(pl.multiple_of(kh * 128, 128), 128)
-    q32 = qrows[pl.ds(pl.multiple_of(ctx * 32, 32), 32), :].reshape(4, 8, 128)
-    nk = nk_v[:, col].astype(F32)
-    nv = nv_v[:, col].astype(F32)
-    s_self = (jnp.sum(q32 * nk[None], axis=-1, keepdims=True) * factor).reshape(32, 1)
-    nv32 = jnp.broadcast_to(nv[None], (4, 8, 128)).reshape(32, 128)
+        acc = jnp.dot(big, vk, preferred_element_type=F32).reshape(16, 8, 128)
+        acc = acc + fresh[k] * nv_v[:, k * 128:(k + 1) * 128].astype(F32)[None]
+        acc_s[k // 2, (k % 2) * 4:(k % 2) * 4 + 4] = acc.reshape(4, 32, 128).astype(BF16)
+    for o in Z_FAR:
+        acc_copy(o).start()
+        drains.append(lambda o=o: acc_copy(o).wait_send())
+    for j in range(2):
+        racc[z, j] = acc_s[j, z]
 
     def wait_stat(o):
-        c = lax.rem(ctx + o, 16)
+        c = lax.rem(z + o, 8)
         rcopy(stat_s, rstat.at[c], ss_s.at[o], ss_r.at[c], me).wait_recv()
 
     def wait_acc(o):
-        c = lax.rem(ctx + o, 16)
-        rcopy(acc_s.at[c], racc.at[c], sa_s.at[o], sa_r.at[c], me).wait_recv()
-
-    loop(1, 16, wait_stat)
-    rt_v[...] = rstat[...].reshape(128, 128).T
-    st = rt_v[pl.ds(pl.multiple_of(lax.rem(ctx, 4) * 32, 32), 32), :]
-    st = pltpu.roll(st, lax.rem(128 - 2 * kh, 128), 1)
-    lane32 = lax.broadcasted_iota(jnp.int32, (32, 128), 1)
-    first = lane32 % 8 == 0
-    tops = jnp.where(first, st, -3e38)
-    high = jnp.maximum(jnp.max(tops, axis=-1, keepdims=True), s_self)
-    wgt = jnp.where(first, jnp.exp(tops - high), 0.0)
-    w_self = jnp.exp(s_self - high)
-    den = jnp.sum(wgt * pltpu.roll(st, 127, 1), axis=-1, keepdims=True) + w_self
-    wgt = wgt / den
-    o_acc = (w_self / den) * nv32
-    loop(1, 16, wait_acc)
-    for s in range(16):
-        o_acc = o_acc + wgt[:, 8 * s:8 * s + 1] * racc[s].astype(F32)
-    ogath[req] = o_acc.astype(BF16)
-
-    def o_copy(dx, dc):
-        peer = at_req(lax.rem(x + dx, 4) * 2 + lax.rem(core + dc, 2))
-        return rcopy(ogath.at[req], ogath.at[req], so_s.at[dx * 2 + dc], so_r.at[req], peer)
-
-    for o in REQ_FAR:
+        c = lax.rem(z + o, 8)
+        rcopy(racc.at[c], racc.at[c], sa_s.at[o], sa_r.at[c], me).wait_recv()
+
+    loop(1, 8, wait_stat)
+    rs = rstat[...]
+    high = jnp.max(rs, axis=0)
+    scale = jnp.exp(rs - high[None])
+    den = jnp.maximum(jnp.sum(scale * pltpu.roll(rs, 7, 1), axis=0), 1e-30)
+    lse = high + jnp.log(den)
+    lse_s[...] = lse
+    flat = (scale / den[None]).reshape(64, 128)
+    rt_v[...] = jnp.concatenate([flat, flat], axis=0).T
+    kz = lax.div(z, 4)
+    rows_z = pl.ds(pl.multiple_of(lax.rem(z, 4) * 32, 32), 32)
+    st = rt_v[rows_z, :]
+    st = jnp.where(kz == 0, st, pltpu.roll(st, 126, 1))
+    loop(1, 8, wait_acc)
+    for j in range(2):
+        part = jnp.zeros((32, 128), F32)
+        for c in range(8):
+            part = part + st[:, 8 * c + 4 * j:8 * c + 4 * j + 1] * racc[c, j].astype(F32)
+        oh_s[j] = part.astype(BF16)
+
+    def h_peer(dx, dc, dh):
+        return lax.rem(yhi + dh, 2), lax.rem(x + dx, 4) * 2 + lax.rem(core + dc, 2)
+
+    def l_copy(dx, dc, dh):
+        h, b = h_peer(dx, dc, dh)
+        return rcopy(lse_s, rl.at[yhi, req], sl_s.at[dh, dx * 2 + dc], sl_r.at[yhi, req], (role, b, h * 8 + z))
+
+    def o_copy(dx, dc, dh):
+        h, b = h_peer(dx, dc, dh)
+        return rcopy(oh_s.at[h], ogath.at[yhi, req], so_s.at[dh, dx * 2 + dc], so_r.at[yhi, req],
+                     (role, b, h * 8 + z))
+
+    pl.semaphore_wait(go, 3)
+    for o in HALF_FAR:
         o_copy(*o).start()
-        drains.append(lambda o=o: o_copy(*o).wait_send())
+        l_copy(*o).start()
+
+    def drain_o():
+        for o in HALF_FAR:
+            o_copy(*o).wait_send()
+            l_copy(*o).wait_send()
+
+    drains.append(drain_o)
+    ogath[yhi, req] = oh_s[yhi]
+    rl[yhi, req] = lse
+
+    def wait_l(o):
+        i = lax.rem(yhi * 8 + req + o, 16)
+        h, b = lax.div(i, 8), lax.rem(i, 8)
+        rcopy(rl.at[h, b], rl.at[h, b], sl_s.at[h, b], sl_r.at[h, b], me).wait_recv()
 
     def wait_o(o):
-        c = lax.rem(req + o, 8)
-        rcopy(ogath.at[c], ogath.at[c], so_s.at[o], so_r.at[c], me).wait_recv()
-
-    loop(1, 8, wait_o)
+        i = lax.rem(yhi * 8 + req + o, 16)
+        h, b = lax.div(i, 8), lax.rem(i, 8)
+        rcopy(ogath.at[h, b], ogath.at[h, b], so_s.at[h, b], so_r.at[h, b], me).wait_recv()
+
+    loop(1, 16, wait_l)
+    gap = rl[1] - rl[0]
+    both = jnp.concatenate(
+        [(1.0 / (1.0 + jnp.exp(gap))).reshape(64, 128), (1.0 / (1.0 + jnp.exp(-gap))).reshape(64, 128)], axis=0)
+    rt_v[...] = both.T
+    st = pltpu.roll(rt_v[rows_z, :], lax.rem(128 - 4 * yhi - 2 * kz, 128), 1)
+    loop(1, 16, wait_o)
+    heads = []
+    for b in range(8):
+        heads.append(st[:, 8 * b:8 * b + 1] * ogath[0, b].astype(F32)
+                     + st[:, 64 + 8 * b:64 + 8 * b + 1] * ogath[1, b].astype(F32))
+    attn = jnp.concatenate(
+        [jnp.concatenate([heads[b][8 * g:8 * g + 8, :] for b in range(8)], axis=0) for g in range(4)],
+        axis=1).astype(BF16)
     local[5].wait()
-    og = ogath[...].astype(F32)
-    attn = jnp.concatenate(
-        [og[:, 8 * g:8 * g + 8, :].reshape(64, 128) for g in range(4)], axis=1).astype(BF16)
     proj = jnp.dot(attn, wo_v[...], preferred_element_type=F32)
     for yy in range(4):
         for zz in range(8):
@@ -457,14 +492,15 @@
             v((8, 8192), BF16), v((8, 128, 512), BF16), v((8, 128, 512), BF16), v((8, 512), BF16),
             v((8, 512), BF16), v((16, 128), BF16), v((512, 1024), BF16), v((64, 128), F32),
             v((1024, 256), BF16), v((256, 128), BF16), v((8192, 256), BF16), v((128, 8192), BF16),
-            v((512, 128), F32), v((16, 32, 128), BF16), v((8, 128), F32), v((16, 32, 128), BF16),
-            v((16, 8, 128), F32), v((128, 128), F32),
-            v((8, 32, 128), BF16), v((4, 8, 16, 128), BF16), v((32, 16, 128), BF16), v((64, 64, 128), BF16),
+            v((2, 8, 32, 128), BF16), v((8, 128), F32), v((8, 2, 32, 128), BF16), v((8, 8, 128), F32),
+            v((128, 128), F32), v((8, 128), F32), v((2, 32, 128), BF16), v((2, 8, 8, 128), F32),
+            v((2, 8, 32, 128), BF16), v((4, 8, 16, 128), BF16), v((32, 16, 128), BF16), v((64, 64, 128), BF16),
             v((8, 128), F32), v((8, 8, 128), F32),
             v((2, 4, 4, 8, 16, 128), BF16), v((4, 4, 8, 16, 128), BF16), v((4, 4, 8, 16, 128), BF16),
             v((4, 4, 8, 16, 128), BF16), v((8, 16, 128), BF16), v((8, 16, 128), BF16),
             dma((13,)),
-            dma((16,)), dma((16,)), dma((16,)), dma((16,)), dma((8,)), dma((8,)), dma((32,)), dma((32,)),
+            pltpu.SemaphoreType.REGULAR, dma((8,)), dma((8,)), dma((8,)), dma((8,)),
+            dma((2, 8)), dma((2, 8)), dma((2, 8)), dma((2, 8)), dma((32,)), dma((32,)),
             dma((8,)), dma((8,)), dma((4, 4)), dma((4, 4)), dma((4,)), dma((4,)),
             dma((8,)), dma((8,)), dma((2,)), dma((4, 4)), dma((4, 4)), dma((16,)),
         ],

time: 65.2 us -> 64.1 us (0.983)
  Pallas kernels: 63.8 us -> 62.7 us
    pallas_call x1, Pallas kernels: 63.8 us -> 62.7 us  [shards(): pl.pallas_call(functools.partial(kernel, None), out_shape=jax.ShapeDtypeS...]
where the time goes in v3:
time: 64.1 us; the launch traced here: 64 us
  Pallas kernels  62.7 us (98%)
  local copies, waits for them, and re-layouts  1.28 us (2%)
    pallas_call x1, Pallas kernels, shards(): pl.pallas_call(functools.partial(kernel, None), out_shape=jax.ShapeDtypeS...  62.7 us

profile of v3, /device:TPU:1, one launch (start us, length us, event | category | flops | bytes accessed | tf_op | source)
XLA Modules:
  0.0 64.0 jit_solution(8090098849369493739)
XLA Ops:
  0.0 62.7 %shard_map.145 = bf16[8,256]{1,0:T(8,128)(2,1)} custom-call(bf16[8,8192]{1,0:T(8,128)(2,1)} %q_h.1, bf16[8,128,512]{2,1,0:T(8,128)(2,1)} %ck_h.1, bf16[8,128,512]{2,1,0:T(8,128)(2,1)} %cv_h.1, bf16[8,512]{1,0:T(8,128)(2,1)} %nk_h.1, bf16[8,512]{1,0:T(8,128)(2,1)} %nv_h.1, s32[8]{0:T(128)} %len_s.1, bf16[64,1024]{1,0:T(8,128)(2,1)} %res_h.1, ...), custom_call_target="tpu_custom_call" | custom-call | tf_op jit(solution)/shard_map/pallas_call | solution.py:486
  62.7 1.3 %copy.17 = bf16[8,256]{1,0:T(8,128)(2,1)} copy(bf16[8,256]{1,0:T(8,128)(2,1)} %shard_map.145) | data formatting | bytes 8192

commit v4 on v3

--- a/solution.py
+++ b/solution.py
@@ -18,6 +18,10 @@
 Z_FAR = (4, 3, 5, 2, 6, 1, 7)
 XY_FAR = ((2, 2), (1, 2), (3, 2), (2, 1), (2, 3), (1, 1), (1, 3), (3, 1), (3, 3),
           (2, 0), (0, 2), (1, 0), (3, 0), (0, 1), (0, 3))
+XY_COLUMN = ((0, 2), (0, 1), (0, 3)) + XY_FAR[:9] + ((2, 0), (1, 0), (3, 0))
+GROUPS = 2
+PER = 8 // GROUPS
+Z_ALL = Z_FAR + (0,)
 YZ_FAR = tuple((dy, dz) for dz in Z_FAR + (0,) for dy in (2, 1, 3, 0) if dy or dz)
 HALF_FAR = tuple((dx, dc, dh) for dh in (1, 0) for dx in (2, 1, 3, 0) for dc in (1, 0) if dx or dc or dh)
 REQ_FAR = ((2, 1), (2, 0), (1, 1), (3, 1), (1, 0), (3, 0), (0, 1))
@@ -46,7 +50,7 @@
     ogath, psend, rpart, xs, ad_s, rad, dbuf, rcore, r1, rx, r3, rz,
     lsem,
     go, sa_s, sa_r, ss_s, ss_r, sl_s, sl_r, so_s, so_r, sp_s, sp_r, sz_s, sz_r, sx_s, sx_r, sc_s, sc_r,
-    sd_s, sd_r, e_c, e_x, e_y, e_z,
+    sd_s, sd_r, ec_s, ec_r, ex_s, ex_r, ez_s, ez_r,
 ):
     role = lax.axis_index("role")
     req = lax.axis_index("req")
@@ -315,7 +319,7 @@
         ref = y_ref(xo * 2 + core, yo)
         rcopy(ref, ref, sx_s.at[dx, dy], sx_r.at[xo, yo], me).wait_recv()
 
-    for o in XY_FAR:
+    for o in XY_COLUMN:
         xy_copy(*o).start()
         drains.append(lambda o=o: xy_copy(*o).wait_send())
 
@@ -373,17 +377,17 @@
         drains.append(lambda o=o: d_copy(*o).wait_send())
     rad[req] = packed
     gu = gate_up(req, xg)
+    for o in (1, 3, 2):
+        b = lax.rem(x + o, 4) * 2 + core
+        for dy in (0, 1, 3, 2):
+            xy_wait(o, dy)
+        c_copy(o).start()
+        drains.append(lambda o=o: c_copy(o).wait_send())
+        s1, xg = block(b)
+        sq = sq + s1
+        gu = gu + gate_up(b, xg)
     for o in (0, 1, 3, 2):
         xo = lax.rem(x + o, 4)
-        if o > 0:
-            b = xo * 2 + core
-            for dy in (0, 1, 3, 2):
-                xy_wait(o, dy)
-            c_copy(o).start()
-            drains.append(lambda o=o: c_copy(o).wait_send())
-            s1, xg = block(b)
-            sq = sq + s1
-            gu = gu + gate_up(b, xg)
         b = xo * 2 + 1 - core
         rcopy(b_ref(b), b_ref(b), sc_s.at[o], sc_r.at[xo], me).wait_recv()
         s1, xg = block(b)
@@ -413,65 +417,70 @@
     hid = (gate / (1.0 + jnp.exp(-gate)) * up).astype(BF16)
 
     local[12].wait()
-    for p in range(32):
-        rr, cc = p // 16, p % 16
-        yy, zz = (cc // 8) * 2 + rr, cc % 8
-        part = jnp.dot(hid, wd_v[:, 256 * p:256 * p + 256], preferred_element_type=F32)
-        for b in range(8):
-            dbuf[b % 2, b // 2, yy, zz] = jnp.concatenate(
-                [part[8 * b:8 * b + 8, 0:128], part[8 * b:8 * b + 8, 128:256]], axis=0).astype(BF16)
-
-    core_copy = rcopy(dbuf.at[1 - core], rcore, e_c.at[0], e_c.at[1], at_req(x * 2 + 1 - core))
-    core_copy.start()
-    drains.append(core_copy.wait_send)
-    core_copy.wait_recv()
-
-    def fold_core(i):
-        r1[i] = (dbuf[core, i].astype(F32) + rcore[i].astype(F32)).astype(BF16)
-
-    loop(0, 4, fold_core)
-
-    def ex_copy(dx, dy):
+
+    def core_copy(g):
+        return rcopy(dbuf.at[1 - core, g], rcore.at[g], ec_s.at[g], ec_r.at[g], at_req(x * 2 + 1 - core))
+
+    def ex_copy(g, dx, dy):
         xo, yo = lax.rem(x + dx, 4), lax.rem(y + dy, 4)
-        return rcopy(r1.at[xo, yo], rx.at[x, y], e_x.at[dx, dy], e_y.at[x, y], at_xy(xo, yo))
-
-    for o in XY_FAR:
-        ex_copy(*o).start()
-        drains.append(lambda o=o: ex_copy(*o).wait_send())
-    rx[x, y] = r1[x, y]
-
-    def wait_ex(o):
-        i = lax.rem(x * 4 + y + o, 16)
-        xo, yo = lax.div(i, 4), lax.rem(i, 4)
-        rcopy(r1.at[xo, yo], rx.at[xo, yo], e_x.at[xo, yo], e_y.at[xo, yo], me).wait_recv()
-
-    loop(1, 16, wait_ex)
-
-    def fold_xy(i):
-        part = rx[0, 0, i].astype(F32)
-        for j in range(1, 16):
-            part = part + rx[j // 4, j % 4, i].astype(F32)
-        r3[i] = part.astype(BF16)
-
-    loop(0, 8, fold_xy)
-
-    def ez_copy(o):
-        zo = lax.rem(z + o, 8)
-        return rcopy(r3.at[zo], rz.at[z], e_z.at[o], e_z.at[8 + z], at_z(zo))
-
-    for o in Z_FAR:
-        ez_copy(o).start()
-        drains.append(lambda o=o: ez_copy(o).wait_send())
-    rz[z] = r3[z]
+        return rcopy(r1.at[g, xo, yo], rx.at[g, x, y], ex_s.at[g, dx, dy], ex_r.at[g, x, y], at_xy(xo, yo))
+
+    def ez_copy(i):
+        zo = lax.rem(z + Z_ALL[i], 8)
+        return rcopy(r3.at[i], rz.at[z], ez_s.at[i], ez_r.at[z], at_z(zo))
+
+    for g in range(GROUPS):
+        for i in range(PER):
+            zo = lax.rem(z + Z_ALL[g * PER + i], 8)
+            for yy in range(4):
+                col = pl.multiple_of(((yy % 2) * 16 + (yy // 2) * 8 + zo) * 256, 256)
+                part = jnp.dot(hid, wd_v[:, pl.ds(col, 256)], preferred_element_type=F32)
+                for b in range(8):
+                    dbuf[b % 2, g, b // 2, yy, i] = jnp.concatenate(
+                        [part[8 * b:8 * b + 8, 0:128], part[8 * b:8 * b + 8, 128:256]], axis=0).astype(BF16)
+        core_copy(g).start()
+        drains.append(lambda g=g: core_copy(g).wait_send())
+
+    for g in range(GROUPS):
+        core_copy(g).wait_recv()
+
+        def fold_core(i):
+            r1[g, i] = (dbuf[core, g, i].astype(F32) + rcore[g, i].astype(F32)).astype(BF16)
+
+        loop(0, 4, fold_core)
+        for o in XY_FAR:
+            ex_copy(g, *o).start()
+            drains.append(lambda g=g, o=o: ex_copy(g, *o).wait_send())
+        rx[g, x, y] = r1[g, x, y]
+
+    own = xs[pl.ds(yz * 2, 2), pl.ds(pl.multiple_of(x * 16, 16), 16), :].astype(F32)
+    own = jnp.where(core == 0, own[:, 0:8, :], own[:, 8:16, :]).reshape(16, 128)
+
+    for g in range(GROUPS):
+        def wait_ex(o):
+            i = lax.rem(x * 4 + y + o, 16)
+            xo, yo = lax.div(i, 4), lax.rem(i, 4)
+            rcopy(rx.at[g, xo, yo], rx.at[g, xo, yo], ex_s.at[g, xo, yo], ex_r.at[g, xo, yo], me).wait_recv()
+
+        loop(1, 16, wait_ex)
+        for i in range(PER):
+            part = rx[g, 0, 0, i].astype(F32)
+            for j in range(1, 16):
+                part = part + rx[g, j // 4, j % 4, i].astype(F32)
+            if Z_ALL[g * PER + i]:
+                r3[g * PER + i] = part.astype(BF16)
+                ez_copy(g * PER + i).start()
+                drains.append(lambda k=g * PER + i: ez_copy(k).wait_send())
+            else:
+                own = own + part
+                rz[z] = jnp.zeros((16, 128), BF16)
 
     def wait_ez(o):
         zo = lax.rem(z + o, 8)
-        rcopy(r3.at[zo], rz.at[zo], e_z.at[o], e_z.at[8 + zo], me).wait_recv()
+        rcopy(rz.at[zo], rz.at[zo], ez_s.at[o], ez_r.at[zo], me).wait_recv()
 
     loop(1, 8, wait_ez)
-    own = xs[pl.ds(yz * 2, 2), pl.ds(pl.multiple_of(x * 16, 16), 16), :].astype(F32)
-    own = jnp.where(core == 0, own[:, 0:8, :], own[:, 8:16, :])
-    res = own.reshape(16, 128) + jnp.sum(rz[...].astype(F32), axis=0)
+    res = own + jnp.sum(rz[...].astype(F32), axis=0)
     out_ref[:, 0:128] = res[0:8, :].astype(BF16)
     out_ref[:, 128:256] = res[8:16, :].astype(BF16)
     finish()
@@ -496,13 +505,14 @@
             v((128, 128), F32), v((8, 128), F32), v((2, 32, 128), BF16), v((2, 8, 8, 128), F32),
             v((2, 8, 32, 128), BF16), v((4, 8, 16, 128), BF16), v((32, 16, 128), BF16), v((64, 64, 128), BF16),
             v((8, 128), F32), v((8, 8, 128), F32),
-            v((2, 4, 4, 8, 16, 128), BF16), v((4, 4, 8, 16, 128), BF16), v((4, 4, 8, 16, 128), BF16),
-            v((4, 4, 8, 16, 128), BF16), v((8, 16, 128), BF16), v((8, 16, 128), BF16),
+            v((2, GROUPS, 4, 4, PER, 16, 128), BF16), v((GROUPS, 4, 4, PER, 16, 128), BF16),
+            v((GROUPS, 4, 4, PER, 16, 128), BF16), v((GROUPS, 4, 4, PER, 16, 128), BF16), v((8, 16, 128), BF16), v((8, 16, 128), BF16),
             dma((13,)),
             pltpu.SemaphoreType.REGULAR, dma((8,)), dma((8,)), dma((8,)), dma((8,)),
             dma((2, 8)), dma((2, 8)), dma((2, 8)), dma((2, 8)), dma((32,)), dma((32,)),
             dma((8,)), dma((8,)), dma((4, 4)), dma((4, 4)), dma((4,)), dma((4,)),
-            dma((8,)), dma((8,)), dma((2,)), dma((4, 4)), dma((4, 4)), dma((16,)),
+            dma((8,)), dma((8,)), dma((GROUPS,)), dma((GROUPS,)),
+            dma((GROUPS, 4, 4)), dma((GROUPS, 4, 4)), dma((8,)), dma((8,)),
         ],
         compiler_params=pltpu.CompilerParams(
             collective_id=0, has_side_effects=True, vmem_limit_bytes=60 * 1024 * 1024),

time: 64.1 us -> 62 us (0.967)
  Pallas kernels: 62.7 us -> 60.6 us
    pallas_call x1, Pallas kernels: 62.7 us -> 60.6 us  [shards(): pl.pallas_call(functools.partial(kernel, None), out_shape=jax.ShapeDtypeS...]
where the time goes in v4:
time: 62 us; the launch traced here: 61.8 us
  Pallas kernels  60.6 us (98%)
  local copies, waits for them, and re-layouts  1.28 us (2%)
    pallas_call x1, Pallas kernels, shards(): pl.pallas_call(functools.partial(kernel, None), out_shape=jax.ShapeDtypeS...  60.6 us
    unnamed x1, local copies, waits for them, and re-layouts  1.28 us

profile of v4, /device:TPU:1, one launch (start us, length us, event | category | flops | bytes accessed | tf_op | source)
XLA Modules:
  0.0 61.8 jit_solution(8049554910270995304)
XLA Ops:
  0.0 60.6 %shard_map.145 = bf16[8,256]{1,0:T(8,128)(2,1)} custom-call(bf16[8,8192]{1,0:T(8,128)(2,1)} %q_h.1, bf16[8,128,512]{2,1,0:T(8,128)(2,1)} %ck_h.1, bf16[8,128,512]{2,1,0:T(8,128)(2,1)} %cv_h.1, bf16[8,512]{1,0:T(8,128)(2,1)} %nk_h.1, bf16[8,512]{1,0:T(8,128)(2,1)} %nv_h.1, s32[8]{0:T(128)} %len_s.1, bf16[64,1024]{1,0:T(8,128)(2,1)} %res_h.1, ...), custom_call_target="tpu_custom_call" | custom-call | tf_op jit(solution)/shard_map/pallas_call | solution.py:495
  60.6 1.3 %copy.17 = bf16[8,256]{1,0:T(8,128)(2,1)} copy(bf16[8,256]{1,0:T(8,128)(2,1)} %shard_map.145) | data formatting | bytes 8192

commit v5 on v4

--- a/solution.py
+++ b/solution.py
@@ -22,6 +22,9 @@
 GROUPS = 2
 PER = 8 // GROUPS
 Z_ALL = Z_FAR + (0,)
+RING = (0, 1, 7, 2, 6, 3, 5, 4)
+RUNS = ((0, 3), (3, 8))
+PLANE = tuple((dx, dc, dy) for dx in (2, 1, 3, 0) for dy in (2, 1, 3, 0) for dc in (1, 0) if dx or dc or dy)
 YZ_FAR = tuple((dy, dz) for dz in Z_FAR + (0,) for dy in (2, 1, 3, 0) if dy or dz)
 HALF_FAR = tuple((dx, dc, dh) for dh in (1, 0) for dx in (2, 1, 3, 0) for dc in (1, 0) if dx or dc or dh)
 REQ_FAR = ((2, 1), (2, 0), (1, 1), (3, 1), (1, 0), (3, 0), (0, 1))
@@ -77,9 +80,9 @@
 
     drains = []
 
-    def finish():
-        for d in drains:
-            d()
+    def drain():
+        while drains:
+            drains.pop(0)()
 
     local = [
         pltpu.make_async_copy(q_h, q_v, lsem.at[0]),
@@ -226,6 +229,7 @@
     for o in HALF_FAR:
         o_copy(*o).start()
         l_copy(*o).start()
+    drain()
 
     def drain_o():
         for o in HALF_FAR:
@@ -273,6 +277,7 @@
 
     for o in YZ_FAR:
         p_copy(*o).start()
+    drain()
 
     def drain_p():
         for o in YZ_FAR:
@@ -289,127 +294,178 @@
     local[6].wait()
     piece = res_v[...].astype(F32) + jnp.sum(rpart[...].astype(F32), axis=0)
     rows_y = pl.ds(pl.multiple_of(y * 16, 16), 16)
-    xs[req * 8 + z, rows_y, :] = piece.astype(BF16)
-
-    def z_ref(i):
-        return xs.at[req * 8 + i, rows_y]
+    xs[req, 0, rows_y, :] = piece.astype(BF16)
 
     def z_copy(o):
-        return rcopy(z_ref(z), z_ref(z), sz_s.at[o], sz_r.at[z], at_z(lax.rem(z + o, 8)))
+        at = RING.index((8 - o) % 8)
+        return rcopy(xs.at[req, 0, rows_y], xs.at[req, at, rows_y], sz_s.at[o], sz_r.at[at],
+                     at_z(lax.rem(z + o, 8)))
+
+    def y_ref(g, b, yo):
+        lo, hi = RUNS[g]
+        return xs.at[b, pl.ds(lo, hi - lo), pl.ds(pl.multiple_of(yo * 16, 16), 16)]
+
+    def xy_copy(g, dx, dy):
+        return rcopy(y_ref(g, req, y), y_ref(g, req, y), sx_s.at[g, dx, dy], sx_r.at[g, x, y],
+                     at_xy(lax.rem(x + dx, 4), lax.rem(y + dy, 4)))
+
+    def xy_wait(g, dx, dy):
+        xo, yo = lax.rem(x + dx, 4), lax.rem(y + dy, 4)
+        ref = y_ref(g, xo * 2 + core, yo)
+        rcopy(ref, ref, sx_s.at[g, dx, dy], sx_r.at[g, xo, yo], me).wait_recv()
+
+    def b_ref(g, b):
+        lo, hi = RUNS[g]
+        return xs.at[b, pl.ds(lo, hi - lo)]
+
+    def c_copy(g, o):
+        xo = lax.rem(x + o, 4)
+        ref = b_ref(g, xo * 2 + core)
+        return rcopy(ref, ref, sc_s.at[g, o], sc_r.at[g, xo], at_req(x * 2 + 1 - core))
+
+    def c_wait(g, o):
+        xo = lax.rem(x + o, 4)
+        ref = b_ref(g, xo * 2 + 1 - core)
+        rcopy(ref, ref, sc_s.at[g, o], sc_r.at[g, xo], me).wait_recv()
 
     for o in Z_FAR:
         z_copy(o).start()
+    for g, (lo, hi) in enumerate(RUNS):
+        for at in range(max(lo, 1), hi):
+            ref = xs.at[req, at, rows_y]
+            rcopy(ref, ref, sz_s.at[at], sz_r.at[at], me).wait_recv()
+        for o in XY_COLUMN:
+            xy_copy(g, *o).start()
+        if g == 0:
+            drain()
+    for o in Z_FAR:
         drains.append(lambda o=o: z_copy(o).wait_send())
-
-    def wait_z(o):
-        c = lax.rem(z + o, 8)
-        rcopy(z_ref(c), z_ref(c), sz_s.at[o], sz_r.at[c], me).wait_recv()
-
-    loop(1, 8, wait_z)
-
-    def y_ref(b, yo):
-        return xs.at[pl.ds(b * 8, 8), pl.ds(pl.multiple_of(yo * 16, 16), 16)]
-
-    def xy_copy(dx, dy):
-        return rcopy(y_ref(req, y), y_ref(req, y), sx_s.at[dx, dy], sx_r.at[x, y],
-                     at_xy(lax.rem(x + dx, 4), lax.rem(y + dy, 4)))
-
-    def xy_wait(dx, dy):
-        xo, yo = lax.rem(x + dx, 4), lax.rem(y + dy, 4)
-        ref = y_ref(xo * 2 + core, yo)
-        rcopy(ref, ref, sx_s.at[dx, dy], sx_r.at[xo, yo], me).wait_recv()
-
-    for o in XY_COLUMN:
-        xy_copy(*o).start()
-        drains.append(lambda o=o: xy_copy(*o).wait_send())
-
-    def b_ref(b):
-        return xs.at[pl.ds(b * 8, 8)]
-
-    def c_copy(o):
-        b = lax.rem(x + o, 4) * 2 + core
-        return rcopy(b_ref(b), b_ref(b), sc_s.at[o], sc_r.at[lax.rem(x + o, 4)], at_req(x * 2 + 1 - core))
-
-    for dy in (1, 3, 2):
-        xy_wait(0, dy)
-    c_copy(0).start()
-    drains.append(lambda: c_copy(0).wait_send())
+    for g in range(len(RUNS)):
+        for o in XY_COLUMN:
+            drains.append(lambda g=g, o=o: xy_copy(g, *o).wait_send())
+    def rows_of(lo, hi, b):
+        return [b * 8 + lax.rem(z + RING[at], 8) for at in range(lo, hi)]
+
+    def gained(xb, chunks):
+        xg = [xb[i] * gain_v[pl.ds(c, 1), :] for i, c in enumerate(chunks)]
+        return jnp.concatenate(xg, axis=1).astype(BF16)
+
+    def block(g, b):
+        lo, hi = RUNS[g]
+        xb = xs[b, lo:hi].astype(F32)
+        sq = jnp.sum(jnp.sum(xb * xb, axis=0), axis=-1, keepdims=True)
+        return sq, gained(xb, rows_of(lo, hi, b))
+
+    def weights(ref, chunks):
+        return jnp.concatenate([ref[pl.ds(pl.multiple_of(c * 128, 128), 128), :] for c in chunks], axis=0)
+
     local[7].wait()
     local[8].wait()
+    owner = lax.div(lane, 16)
+
+    def tenants(first):
+        t = jnp.zeros((8, 128), jnp.int32)
+        for r in range(8):
+            t = jnp.where(sub == r, ten_s[first + r], t)
+        return t
+
+    def spread(v):
+        v = v + pltpu.roll(v, 64, 1)
+        v = v + pltpu.roll(v, 32, 1)
+        return v + pltpu.roll(v, 16, 1)
+
+    mid = jnp.dot(gained(xs[req, :, rows_y, :].astype(F32), rows_of(0, 8, req)), weights(ad_v, rows_of(0, 8, 0)),
+                  preferred_element_type=F32)
+    for i in range(2):
+        t = tenants(y * 16 + 8 * i)
+        v = (jnp.where(owner == t, mid[8 * i:8 * i + 8, 0:128], 0.0)
+             + jnp.where(owner + 8 == t, mid[8 * i:8 * i + 8, 128:256], 0.0))
+        ad_s[i:i + 1, :] = jnp.sum(jnp.where(owner == sub, spread(v), 0.0), axis=0, keepdims=True)
+
+    def rad_ref(b, yo):
+        return rad.at[b, pl.ds(2 * yo, 2)]
+
+    def d_copy(dx, dc, dy):
+        yo, b = lax.rem(y + dy, 4), lax.rem(x + dx, 4) * 2 + lax.rem(core + dc, 2)
+        return rcopy(ad_s, rad_ref(req, y), sd_s.at[dx * 2 + dc, dy], sd_r.at[req, y],
+                     (lax.rem(yo, 2), b, lax.div(yo, 2) * 8 + z))
+
+    for o in PLANE:
+        d_copy(*o).start()
+        drains.append(lambda o=o: d_copy(*o).wait_send())
+    rad[req, pl.ds(2 * y, 2), :] = ad_s[...]
+
+    def wait_d(o):
+        i = lax.rem(req * 4 + y + o, 32)
+        ref = rad_ref(lax.div(i, 4), lax.rem(i, 4))
+        rcopy(ref, ref, sd_s.at[0, 0], sd_r.at[lax.div(i, 4), lax.rem(i, 4)], me).wait_recv()
+
     local[10].wait()
     local[11].wait()
 
-    def block(b):
-        xb = xs[pl.ds(b * 8, 8)].astype(F32)
-        sq = jnp.sum(jnp.sum(xb * xb, axis=0), axis=-1, keepdims=True)
-        xg = xb * gain_v[pl.ds(pl.multiple_of(b * 8, 8), 8), :][:, None, :]
-        xg = jnp.concatenate([xg[i] for i in range(8)], axis=1).astype(BF16)
-        return sq, xg
-
-    def gate_up(b, xg):
-        rows = pl.ds(pl.multiple_of(b * 1024, 1024), 1024)
-        return jnp.dot(xg, wgu_v[rows, :], preferred_element_type=F32)
-
-    sq, xg = block(req)
-    mid = jnp.dot(xg, ad_v[...], preferred_element_type=F32)
-    owner = lax.div(lane, 16)
-    tens = []
-    packed = jnp.zeros((8, 128), F32)
-    for i in range(8):
-        t = jnp.zeros((8, 128), jnp.int32)
-        for r in range(8):
-            t = jnp.where(sub == r, ten_s[8 * i + r], t)
-        tens.append(t)
-        v = (jnp.where(owner == t, mid[8 * i:8 * i + 8, 0:128], 0.0)
-             + jnp.where(owner + 8 == t, mid[8 * i:8 * i + 8, 128:256], 0.0))
-        v = v + pltpu.roll(v, 64, 1)
-        v = v + pltpu.roll(v, 32, 1)
-        v = v + pltpu.roll(v, 16, 1)
-        packed = jnp.where(owner == i, v, packed)
-    ad_s[...] = packed
-
-    def d_copy(dx, dc):
-        peer = at_req(lax.rem(x + dx, 4) * 2 + lax.rem(core + dc, 2))
-        return rcopy(ad_s, rad.at[req], sd_s.at[dx * 2 + dc], sd_r.at[req], peer)
-
-    for o in REQ_FAR:
-        d_copy(*o).start()
-        drains.append(lambda o=o: d_copy(*o).wait_send())
-    rad[req] = packed
-    gu = gate_up(req, xg)
+    def gate_up(g, b, xg):
+        return jnp.dot(xg, weights(wgu_v, rows_of(*RUNS[g], b)), preferred_element_type=F32)
+
+    def forward(g, o):
+        c_copy(g, o).start()
+        drains.append(lambda: c_copy(g, o).wait_send())
+
+    sq = jnp.zeros((64, 1), F32)
+    gu = jnp.zeros((64, 256), F32)
+    last = len(RUNS) - 1
+    for g in range(len(RUNS)):
+        for dy in (1, 3, 2):
+            xy_wait(g, 0, dy)
+        forward(g, 0)
+        s1, xg = block(g, req)
+        sq = sq + s1
+        own_xg = xg
+        if g == last:
+            break
+        gu = gu + gate_up(g, req, xg)
+        for o in (1, 3, 2):
+            for dy in (0, 1, 3, 2):
+                xy_wait(g, o, dy)
+            forward(g, o)
+        for o in (1, 3, 2):
+            b = lax.rem(x + o, 4) * 2 + core
+            s1, xg = block(g, b)
+            sq = sq + s1
+            gu = gu + gate_up(g, b, xg)
+        for o in (0, 1, 3, 2) if g else ():
+            c_wait(g - 1, o)
+            b = lax.rem(x + o, 4) * 2 + 1 - core
+            s1, xg = block(g - 1, b)
+            sq = sq + s1
+            gu = gu + gate_up(g - 1, b, xg)
+    gu = gu + gate_up(last, req, own_xg)
+    for o in (1, 3, 2):
+        for dy in (0, 1, 3, 2):
+            xy_wait(last, o, dy)
+        forward(last, o)
     for o in (1, 3, 2):
         b = lax.rem(x + o, 4) * 2 + core
-        for dy in (0, 1, 3, 2):
-            xy_wait(o, dy)
-        c_copy(o).start()
-        drains.append(lambda o=o: c_copy(o).wait_send())
-        s1, xg = block(b)
+        s1, xg = block(last, b)
         sq = sq + s1
-        gu = gu + gate_up(b, xg)
-    for o in (0, 1, 3, 2):
-        xo = lax.rem(x + o, 4)
-        b = xo * 2 + 1 - core
-        rcopy(b_ref(b), b_ref(b), sc_s.at[o], sc_r.at[xo], me).wait_recv()
-        s1, xg = block(b)
-        sq = sq + s1
-        gu = gu + gate_up(b, xg)
-
-    def wait_d(o):
-        c = lax.rem(req + o, 8)
-        rcopy(ad_s, rad.at[c], sd_s.at[o], sd_r.at[c], me).wait_recv()
-
-    loop(1, 8, wait_d)
+        gu = gu + gate_up(last, b, xg)
+    for g in range(max(last - 1, 0), last + 1):
+        for o in (0, 1, 3, 2):
+            c_wait(g, o)
+            b = lax.rem(x + o, 4) * 2 + 1 - core
+            s1, xg = block(g, b)
+            sq = sq + s1
+            gu = gu + gate_up(g, b, xg)
+
+    loop(1, 32, wait_d)
     inv = lax.rsqrt(sq * (1.0 / 8192.0) + EPS)
     allmid = jnp.sum(rad[...], axis=0)
     chosen = []
     for i in range(8):
-        v = jnp.where(owner == i, allmid, 0.0)
-        v = v + pltpu.roll(v, 64, 1)
-        v = v + pltpu.roll(v, 32, 1)
-        v = v + pltpu.roll(v, 16, 1)
+        t = tenants(8 * i)
+        v = spread(jnp.where(owner == sub, jnp.broadcast_to(allmid[i:i + 1, :], (8, 128)), 0.0))
         v = v * inv[8 * i:8 * i + 8]
         chosen.append(jnp.concatenate(
-            [jnp.where(owner == tens[i], v, 0.0), jnp.where(owner + 8 == tens[i], v, 0.0)], axis=1))
+            [jnp.where(owner == t, v, 0.0), jnp.where(owner + 8 == t, v, 0.0)], axis=1))
     local[9].wait()
     lowrank = jnp.dot(jnp.concatenate(chosen, axis=0).astype(BF16), tu_v[...], preferred_element_type=F32)
     gate = gu[:, 0:128] * inv
@@ -452,9 +508,20 @@
             ex_copy(g, *o).start()
             drains.append(lambda g=g, o=o: ex_copy(g, *o).wait_send())
         rx[g, x, y] = r1[g, x, y]
-
-    own = xs[pl.ds(yz * 2, 2), pl.ds(pl.multiple_of(x * 16, 16), 16), :].astype(F32)
-    own = jnp.where(core == 0, own[:, 0:8, :], own[:, 8:16, :]).reshape(16, 128)
+        if g == 0:
+            late, drains[:] = drains[-16:], drains[:-16]
+            drain()
+            drains.extend(late)
+
+    own = []
+    for h in range(2):
+        c = yz * 2 + h
+        away = lax.rem(lax.rem(c, 8) + 8 - z, 8)
+        past = lax.div(away, 5)
+        at = (1 - past) * (2 * away - 1) + past * (16 - 2 * away) + lax.div(8 - away, 8)
+        t = xs[lax.div(c, 8), at, pl.ds(pl.multiple_of(x * 16, 16), 16), :].astype(F32)
+        own.append(jnp.where(core == 0, t[0:8, :], t[8:16, :]))
+    own = jnp.concatenate(own, axis=0)
 
     for g in range(GROUPS):
         def wait_ex(o):
@@ -475,6 +542,10 @@
                 own = own + part
                 rz[z] = jnp.zeros((16, 128), BF16)
 
+    late, drains[:] = drains[-7:], drains[:-7]
+    drain()
+    drains.extend(late)
+
     def wait_ez(o):
         zo = lax.rem(z + o, 8)
         rcopy(rz.at[zo], rz.at[zo], ez_s.at[o], ez_r.at[zo], me).wait_recv()
@@ -483,7 +554,7 @@
     res = own + jnp.sum(rz[...].astype(F32), axis=0)
     out_ref[:, 0:128] = res[0:8, :].astype(BF16)
     out_ref[:, 128:256] = res[8:16, :].astype(BF16)
-    finish()
+    drain()
 
 
 def shards(query, cache_keys, cache_values, new_keys, new_values, lengths, residual_in, out_proj,
@@ -503,15 +574,16 @@
             v((1024, 256), BF16), v((256, 128), BF16), v((8192, 256), BF16), v((128, 8192), BF16),
             v((2, 8, 32, 128), BF16), v((8, 128), F32), v((8, 2, 32, 128), BF16), v((8, 8, 128), F32),
             v((128, 128), F32), v((8, 128), F32), v((2, 32, 128), BF16), v((2, 8, 8, 128), F32),
-            v((2, 8, 32, 128), BF16), v((4, 8, 16, 128), BF16), v((32, 16, 128), BF16), v((64, 64, 128), BF16),
-            v((8, 128), F32), v((8, 8, 128), F32),
+            v((2, 8, 32, 128), BF16), v((4, 8, 16, 128), BF16), v((32, 16, 128), BF16), v((8, 8, 64, 128), BF16),
+            v((2, 128), F32), v((8, 8, 128), F32),
             v((2, GROUPS, 4, 4, PER, 16, 128), BF16), v((GROUPS, 4, 4, PER, 16, 128), BF16),
             v((GROUPS, 4, 4, PER, 16, 128), BF16), v((GROUPS, 4, 4, PER, 16, 128), BF16), v((8, 16, 128), BF16), v((8, 16, 128), BF16),
             dma((13,)),
             pltpu.SemaphoreType.REGULAR, dma((8,)), dma((8,)), dma((8,)), dma((8,)),
             dma((2, 8)), dma((2, 8)), dma((2, 8)), dma((2, 8)), dma((32,)), dma((32,)),
-            dma((8,)), dma((8,)), dma((4, 4)), dma((4, 4)), dma((4,)), dma((4,)),
-            dma((8,)), dma((8,)), dma((GROUPS,)), dma((GROUPS,)),
+            dma((8,)), dma((8,)), dma((len(RUNS), 4, 4)), dma((len(RUNS), 4, 4)),
+            dma((len(RUNS), 4)), dma((len(RUNS), 4)),
+            dma((8, 4)), dma((8, 4)), dma((GROUPS,)), dma((GROUPS,)),
             dma((GROUPS, 4, 4)), dma((GROUPS, 4, 4)), dma((8,)), dma((8,)),
         ],
         compiler_params=pltpu.CompilerParams(

time: 62 us -> 59.5 us (0.960)
  Pallas kernels: 60.6 us -> 58.1 us
    pallas_call x1, Pallas kernels: 60.6 us -> 58.1 us  [shards(): pl.pallas_call(functools.partial(kernel, None), out_shape=jax.ShapeDtypeS...]
where the time goes in v5:
time: 59.5 us; the launch traced here: 59.4 us
  Pallas kernels  58.1 us (98%)
  local copies, waits for them, and re-layouts  1.28 us (2%)
    pallas_call x1, Pallas kernels, shards(): pl.pallas_call(functools.partial(kernel, None), out_shape=jax.ShapeDtypeS...  58.1 us
    unnamed x1, local copies, waits for them, and re-layouts  1.28 us

profile of v5, /device:TPU:1, one launch (start us, length us, event | category | flops | bytes accessed | tf_op | source)
XLA Modules:
  0.0 59.4 jit_solution(12344460976450635995)
XLA Ops:
  0.0 58.1 %shard_map.145 = bf16[8,256]{1,0:T(8,128)(2,1)} custom-call(bf16[8,8192]{1,0:T(8,128)(2,1)} %q_h.1, bf16[8,128,512]{2,1,0:T(8,128)(2,1)} %ck_h.1, bf16[8,128,512]{2,1,0:T(8,128)(2,1)} %cv_h.1, bf16[8,512]{1,0:T(8,128)(2,1)} %nk_h.1, bf16[8,512]{1,0:T(8,128)(2,1)} %nv_h.1, s32[8]{0:T(128)} %len_s.1, bf16[64,1024]{1,0:T(8,128)(2,1)} %res_h.1, ...), custom_call_target="tpu_custom_call" | custom-call | tf_op jit(solution)/shard_map/pallas_call | solution.py:566
  58.1 1.3 %copy.17 = bf16[8,256]{1,0:T(8,128)(2,1)} copy(bf16[8,256]{1,0:T(8,128)(2,1)} %shard_map.145) | data formatting | bytes 8192

commit v6 on v5

--- a/solution.py
+++ b/solution.py
@@ -19,8 +19,7 @@
 XY_FAR = ((2, 2), (1, 2), (3, 2), (2, 1), (2, 3), (1, 1), (1, 3), (3, 1), (3, 3),
           (2, 0), (0, 2), (1, 0), (3, 0), (0, 1), (0, 3))
 XY_COLUMN = ((0, 2), (0, 1), (0, 3)) + XY_FAR[:9] + ((2, 0), (1, 0), (3, 0))
-GROUPS = 2
-PER = 8 // GROUPS
+PARTS = ((0, 3), (3, 6), (6, 8))
 Z_ALL = Z_FAR + (0,)
 RING = (0, 1, 7, 2, 6, 3, 5, 4)
 RUNS = ((0, 3), (3, 8))
@@ -49,10 +48,10 @@
     q_h, ck_h, cv_h, nk_h, nv_h, len_s, res_h, wo_h, gain_h, ad_h, tu_h, ten_s, wg_h, wu_h, wd_h,
     out_ref,
     q_v, ck_v, cv_v, nk_v, nv_v, res_v, wo_v, gain_v, ad_v, tu_v, wgu_v, wd_v,
-    acc_s, stat_s, racc, rstat, rt_v, lse_s, oh_s, rl,
+    acc_s, stat_s, racc, rstat, rt_v, lse_s, oh_s,
     ogath, psend, rpart, xs, ad_s, rad, dbuf, rcore, r1, rx, r3, rz,
     lsem,
-    go, sa_s, sa_r, ss_s, ss_r, sl_s, sl_r, so_s, so_r, sp_s, sp_r, sz_s, sz_r, sx_s, sx_r, sc_s, sc_r,
+    go, sa_s, sa_r, ss_s, ss_r, so_s, so_r, sp_s, sp_r, sz_s, sz_r, sx_s, sx_r, sc_s, sc_r,
     sd_s, sd_r, ec_s, ec_r, ex_s, ex_r, ez_s, ez_r,
 ):
     role = lax.axis_index("role")
@@ -77,6 +76,18 @@
 
     def at_z(i):
         return (role, req, yhi * 8 + i)
+
+    barrier = pltpu.get_barrier_semaphore()
+
+    def greet(dev):
+        pl.semaphore_signal(barrier, inc=1, device_id=dev, device_id_type=MESH)
+
+    for o in Z_FAR:
+        greet(at_z(lax.rem(z + o, 8)))
+    for dx, dc in REQ_FAR:
+        greet(at_req(lax.rem(x + dx, 4) * 2 + lax.rem(core + dc, 2)))
+    for o in (2, 1, 3):
+        greet(at_y(lax.rem(y + o, 4)))
 
     drains = []
 
@@ -104,18 +115,6 @@
     ]
     for i in (0, 1, 3, 2, 4, 5, 6, 7, 8, 9, 10, 11, 12):
         local[i].start()
-
-    barrier = pltpu.get_barrier_semaphore()
-
-    def greet(dev):
-        pl.semaphore_signal(barrier, inc=1, device_id=dev, device_id_type=MESH)
-
-    for o in Z_FAR:
-        greet(at_z(lax.rem(z + o, 8)))
-    for dx, dc in REQ_FAR:
-        greet(at_req(lax.rem(x + dx, 4) * 2 + lax.rem(core + dc, 2)))
-    for o in (2, 1, 3):
-        greet(at_y(lax.rem(y + o, 4)))
 
     factor = 1.0 / math.sqrt(HD)
     sub = lax.broadcasted_iota(jnp.int32, (8, 128), 0)
@@ -162,9 +161,12 @@
     def stat_copy(o):
         return rcopy(stat_s, rstat.at[z], ss_s.at[o], ss_r.at[z], at_z(lax.rem(z + o, 8)))
 
-    def acc_copy(o):
+    def half(n):
+        return 1 - yhi if n == 0 else yhi
+
+    def acc_copy(n, o):
         zo = lax.rem(z + o, 8)
-        return rcopy(acc_s.at[:, zo], racc.at[z], sa_s.at[o], sa_r.at[z], at_z(zo))
+        return rcopy(acc_s.at[half(n), zo], racc.at[z, half(n)], sa_s.at[n, o], sa_r.at[n, z], at_z(zo))
 
     for o in Z_FAR:
         stat_copy(o).start()
@@ -179,19 +181,16 @@
         acc = jnp.dot(big, vk, preferred_element_type=F32).reshape(16, 8, 128)
         acc = acc + fresh[k] * nv_v[:, k * 128:(k + 1) * 128].astype(F32)[None]
         acc_s[k // 2, (k % 2) * 4:(k % 2) * 4 + 4] = acc.reshape(4, 32, 128).astype(BF16)
-    for o in Z_FAR:
-        acc_copy(o).start()
-        drains.append(lambda o=o: acc_copy(o).wait_send())
+    for n in range(2):
+        for o in Z_FAR:
+            acc_copy(n, o).start()
+            drains.append(lambda n=n, o=o: acc_copy(n, o).wait_send())
     for j in range(2):
         racc[z, j] = acc_s[j, z]
 
     def wait_stat(o):
         c = lax.rem(z + o, 8)
         rcopy(stat_s, rstat.at[c], ss_s.at[o], ss_r.at[c], me).wait_recv()
-
-    def wait_acc(o):
-        c = lax.rem(z + o, 8)
-        rcopy(racc.at[c], racc.at[c], sa_s.at[o], sa_r.at[c], me).wait_recv()
 
     loop(1, 8, wait_stat)
     rs = rstat[...]
@@ -206,61 +205,60 @@
     rows_z = pl.ds(pl.multiple_of(lax.rem(z, 4) * 32, 32), 32)
     st = rt_v[rows_z, :]
     st = jnp.where(kz == 0, st, pltpu.roll(st, 126, 1))
-    loop(1, 8, wait_acc)
-    for j in range(2):
-        part = jnp.zeros((32, 128), F32)
-        for c in range(8):
-            part = part + st[:, 8 * c + 4 * j:8 * c + 4 * j + 1] * racc[c, j].astype(F32)
-        oh_s[j] = part.astype(BF16)
-
     def h_peer(dx, dc, dh):
         return lax.rem(yhi + dh, 2), lax.rem(x + dx, 4) * 2 + lax.rem(core + dc, 2)
-
-    def l_copy(dx, dc, dh):
-        h, b = h_peer(dx, dc, dh)
-        return rcopy(lse_s, rl.at[yhi, req], sl_s.at[dh, dx * 2 + dc], sl_r.at[yhi, req], (role, b, h * 8 + z))
 
     def o_copy(dx, dc, dh):
         h, b = h_peer(dx, dc, dh)
         return rcopy(oh_s.at[h], ogath.at[yhi, req], so_s.at[dh, dx * 2 + dc], so_r.at[yhi, req],
                      (role, b, h * 8 + z))
 
-    pl.semaphore_wait(go, 3)
-    for o in HALF_FAR:
-        o_copy(*o).start()
-        l_copy(*o).start()
+    for n in range(2):
+        def wait_acc(o):
+            c = lax.rem(z + o, 8)
+            ref = racc.at[c, half(n)]
+            rcopy(ref, ref, sa_s.at[n, o], sa_r.at[n, c], me).wait_recv()
+
+        loop(1, 8, wait_acc)
+        mine = jnp.where(half(n) == 0, st, pltpu.roll(st, 124, 1))
+        part = jnp.zeros((32, 128), F32)
+        for c in range(8):
+            part = part + mine[:, 8 * c:8 * c + 1] * racc[c, half(n)].astype(F32)
+        row = lse_s[pl.ds(4 * half(n) + 2 * kz, 1), :]
+        head = row.astype(BF16).astype(F32)
+        middle = (row - head).astype(BF16).astype(F32)
+        oh_s[half(n)] = jnp.concatenate(
+            [part, head, middle, row - head - middle, jnp.zeros((13, 128), F32)], axis=0).astype(BF16)
+        if n == 0:
+            pl.semaphore_wait(go, 3)
+        for o in HALF_FAR:
+            if o[2] == 1 - n:
+                o_copy(*o).start()
     drain()
 
     def drain_o():
         for o in HALF_FAR:
             o_copy(*o).wait_send()
-            l_copy(*o).wait_send()
 
     drains.append(drain_o)
     ogath[yhi, req] = oh_s[yhi]
-    rl[yhi, req] = lse
-
-    def wait_l(o):
-        i = lax.rem(yhi * 8 + req + o, 16)
-        h, b = lax.div(i, 8), lax.rem(i, 8)
-        rcopy(rl.at[h, b], rl.at[h, b], sl_s.at[h, b], sl_r.at[h, b], me).wait_recv()
 
     def wait_o(o):
         i = lax.rem(yhi * 8 + req + o, 16)
         h, b = lax.div(i, 8), lax.rem(i, 8)
         rcopy(ogath.at[h, b], ogath.at[h, b], so_s.at[h, b], so_r.at[h, b], me).wait_recv()
 
-    loop(1, 16, wait_l)
-    gap = rl[1] - rl[0]
+    loop(1, 16, wait_o)
+    logs = jnp.sum(ogath[:, :, 32:48, :].astype(F32), axis=2)
+    gap = logs[1] - logs[0]
     both = jnp.concatenate(
-        [(1.0 / (1.0 + jnp.exp(gap))).reshape(64, 128), (1.0 / (1.0 + jnp.exp(-gap))).reshape(64, 128)], axis=0)
+        [1.0 / (1.0 + jnp.exp(gap)), 1.0 / (1.0 + jnp.exp(-gap)), jnp.zeros((112, 128), F32)], axis=0)
     rt_v[...] = both.T
-    st = pltpu.roll(rt_v[rows_z, :], lax.rem(128 - 4 * yhi - 2 * kz, 128), 1)
-    loop(1, 16, wait_o)
+    st = rt_v[rows_z, :]
     heads = []
     for b in range(8):
-        heads.append(st[:, 8 * b:8 * b + 1] * ogath[0, b].astype(F32)
-                     + st[:, 64 + 8 * b:64 + 8 * b + 1] * ogath[1, b].astype(F32))
+        heads.append(st[:, b:b + 1] * ogath[0, b, 0:32].astype(F32)
+                     + st[:, 8 + b:9 + b] * ogath[1, b, 0:32].astype(F32))
     attn = jnp.concatenate(
         [jnp.concatenate([heads[b][8 * g:8 * g + 8, :] for b in range(8)], axis=0) for g in range(4)],
         axis=1).astype(BF16)
@@ -474,40 +472,46 @@
 
     local[12].wait()
 
+    def part_of(g):
+        lo, hi = PARTS[g]
+        return pl.ds(lo, hi - lo)
+
     def core_copy(g):
-        return rcopy(dbuf.at[1 - core, g], rcore.at[g], ec_s.at[g], ec_r.at[g], at_req(x * 2 + 1 - core))
+        return rcopy(dbuf.at[1 - core, :, :, part_of(g)], rcore.at[:, :, part_of(g)], ec_s.at[g], ec_r.at[g],
+                     at_req(x * 2 + 1 - core))
 
     def ex_copy(g, dx, dy):
         xo, yo = lax.rem(x + dx, 4), lax.rem(y + dy, 4)
-        return rcopy(r1.at[g, xo, yo], rx.at[g, x, y], ex_s.at[g, dx, dy], ex_r.at[g, x, y], at_xy(xo, yo))
+        return rcopy(r1.at[xo, yo, part_of(g)], rx.at[x, y, part_of(g)], ex_s.at[g, dx, dy], ex_r.at[g, x, y],
+                     at_xy(xo, yo))
 
     def ez_copy(i):
         zo = lax.rem(z + Z_ALL[i], 8)
         return rcopy(r3.at[i], rz.at[z], ez_s.at[i], ez_r.at[z], at_z(zo))
 
-    for g in range(GROUPS):
-        for i in range(PER):
-            zo = lax.rem(z + Z_ALL[g * PER + i], 8)
+    for g, (lo, hi) in enumerate(PARTS):
+        for i in range(lo, hi):
+            zo = lax.rem(z + Z_ALL[i], 8)
             for yy in range(4):
                 col = pl.multiple_of(((yy % 2) * 16 + (yy // 2) * 8 + zo) * 256, 256)
                 part = jnp.dot(hid, wd_v[:, pl.ds(col, 256)], preferred_element_type=F32)
                 for b in range(8):
-                    dbuf[b % 2, g, b // 2, yy, i] = jnp.concatenate(
+                    dbuf[b % 2, b // 2, yy, i] = jnp.concatenate(
                         [part[8 * b:8 * b + 8, 0:128], part[8 * b:8 * b + 8, 128:256]], axis=0).astype(BF16)
         core_copy(g).start()
         drains.append(lambda g=g: core_copy(g).wait_send())
 
-    for g in range(GROUPS):
+    for g, (lo, hi) in enumerate(PARTS):
         core_copy(g).wait_recv()
 
         def fold_core(i):
-            r1[g, i] = (dbuf[core, g, i].astype(F32) + rcore[g, i].astype(F32)).astype(BF16)
+            r1[i, :, lo:hi] = (dbuf[core, i, :, lo:hi].astype(F32) + rcore[i, :, lo:hi].astype(F32)).astype(BF16)
 
         loop(0, 4, fold_core)
         for o in XY_FAR:
             ex_copy(g, *o).start()
             drains.append(lambda g=g, o=o: ex_copy(g, *o).wait_send())
-        rx[g, x, y] = r1[g, x, y]
+        rx[x, y, lo:hi] = r1[x, y, lo:hi]
         if g == 0:
             late, drains[:] = drains[-16:], drains[:-16]
             drain()
@@ -523,21 +527,22 @@
         own.append(jnp.where(core == 0, t[0:8, :], t[8:16, :]))
     own = jnp.concatenate(own, axis=0)
 
-    for g in range(GROUPS):
+    for g, (lo, hi) in enumerate(PARTS):
         def wait_ex(o):
             i = lax.rem(x * 4 + y + o, 16)
             xo, yo = lax.div(i, 4), lax.rem(i, 4)
-            rcopy(rx.at[g, xo, yo], rx.at[g, xo, yo], ex_s.at[g, xo, yo], ex_r.at[g, xo, yo], me).wait_recv()
+            ref = rx.at[xo, yo, part_of(g)]
+            rcopy(ref, ref, ex_s.at[g, xo, yo], ex_r.at[g, xo, yo], me).wait_recv()
 
         loop(1, 16, wait_ex)
-        for i in range(PER):
-            part = rx[g, 0, 0, i].astype(F32)
+        for i in range(lo, hi):
+            part = rx[0, 0, i].astype(F32)
             for j in range(1, 16):
-                part = part + rx[g, j // 4, j % 4, i].astype(F32)
-            if Z_ALL[g * PER + i]:
-                r3[g * PER + i] = part.astype(BF16)
-                ez_copy(g * PER + i).start()
-                drains.append(lambda k=g * PER + i: ez_copy(k).wait_send())
+                part = part + rx[j // 4, j % 4, i].astype(F32)
+            if Z_ALL[i]:
+                r3[i] = part.astype(BF16)
+                ez_copy(i).start()
+                drains.append(lambda k=i: ez_copy(k).wait_send())
             else:
                 own = own + part
                 rz[z] = jnp.zeros((16, 128), BF16)
@@ -552,8 +557,8 @@
 
     loop(1, 8, wait_ez)
     res = own + jnp.sum(rz[...].astype(F32), axis=0)
-    out_ref[:, 0:128] = res[0:8, :].astype(BF16)
-    out_ref[:, 128:256] = res[8:16, :].astype(BF16)
+    out_ref[:, 0:128] = res[0:8, :]
+    out_ref[:, 128:256] = res[8:16, :]
     drain()
 
 
@@ -565,7 +570,7 @@
     dma = pltpu.SemaphoreType.DMA
     return pl.pallas_call(
         functools.partial(kernel, None),
-        out_shape=jax.ShapeDtypeStruct((8, 256), BF16),
+        out_shape=jax.ShapeDtypeStruct((8, 256), F32),
         in_specs=[hbm, hbm, hbm, hbm, hbm, smem, hbm, hbm, hbm, hbm, hbm, smem, hbm, hbm, hbm],
         out_specs=pl.BlockSpec(memory_space=pltpu.VMEM),
         scratch_shapes=[
@@ -573,23 +578,23 @@
             v((8, 512), BF16), v((16, 128), BF16), v((512, 1024), BF16), v((64, 128), F32),
             v((1024, 256), BF16), v((256, 128), BF16), v((8192, 256), BF16), v((128, 8192), BF16),
             v((2, 8, 32, 128), BF16), v((8, 128), F32), v((8, 2, 32, 128), BF16), v((8, 8, 128), F32),
-            v((128, 128), F32), v((8, 128), F32), v((2, 32, 128), BF16), v((2, 8, 8, 128), F32),
-            v((2, 8, 32, 128), BF16), v((4, 8, 16, 128), BF16), v((32, 16, 128), BF16), v((8, 8, 64, 128), BF16),
+            v((128, 128), F32), v((8, 128), F32), v((2, 48, 128), BF16),
+            v((2, 8, 48, 128), BF16), v((4, 8, 16, 128), BF16), v((32, 16, 128), BF16), v((8, 8, 64, 128), BF16),
             v((2, 128), F32), v((8, 8, 128), F32),
-            v((2, GROUPS, 4, 4, PER, 16, 128), BF16), v((GROUPS, 4, 4, PER, 16, 128), BF16),
-            v((GROUPS, 4, 4, PER, 16, 128), BF16), v((GROUPS, 4, 4, PER, 16, 128), BF16), v((8, 16, 128), BF16), v((8, 16, 128), BF16),
+            v((2, 4, 4, 8, 16, 128), BF16), v((4, 4, 8, 16, 128), BF16), v((4, 4, 8, 16, 128), BF16),
+            v((4, 4, 8, 16, 128), BF16), v((8, 16, 128), BF16), v((8, 16, 128), BF16),
             dma((13,)),
-            pltpu.SemaphoreType.REGULAR, dma((8,)), dma((8,)), dma((8,)), dma((8,)),
-            dma((2, 8)), dma((2, 8)), dma((2, 8)), dma((2, 8)), dma((32,)), dma((32,)),
+            pltpu.SemaphoreType.REGULAR, dma((2, 8)), dma((2, 8)), dma((8,)), dma((8,)),
+            dma((2, 8)), dma((2, 8)), dma((32,)), dma((32,)),
             dma((8,)), dma((8,)), dma((len(RUNS), 4, 4)), dma((len(RUNS), 4, 4)),
             dma((len(RUNS), 4)), dma((len(RUNS), 4)),
-            dma((8, 4)), dma((8, 4)), dma((GROUPS,)), dma((GROUPS,)),
-            dma((GROUPS, 4, 4)), dma((GROUPS, 4, 4)), dma((8,)), dma((8,)),
+            dma((8, 4)), dma((8, 4)), dma((len(PARTS),)), dma((len(PARTS),)),
+            dma((len(PARTS), 4, 4)), dma((len(PARTS), 4, 4)), dma((8,)), dma((8,)),
         ],
         compiler_params=pltpu.CompilerParams(
             collective_id=0, has_side_effects=True, vmem_limit_bytes=60 * 1024 * 1024),
     )(query, cache_keys, cache_values, new_keys, new_values, lengths, residual_in, out_proj,
-      norm_gain.reshape(64, 128), adapter_down, tenant_adapter_up_matrix, tenant, w_gate, w_up, w_down)
+      norm_gain.reshape(64, 128), adapter_down, tenant_adapter_up_matrix, tenant, w_gate, w_up, w_down).astype(BF16)
 
 
 def solution(mesh):

time: 59.5 us -> 58.8 us (0.988)
  other arithmetic: 0 us -> 1.29 us
  local copies, waits for them, and re-layouts: 1.28 us -> 0 us
  Pallas kernels: 58.1 us -> 57.3 us
    convert_element_type x0 -> x1, other arithmetic: none -> 1.29 us  [shards(): return pl.pallas_call(functools.partial(kernel, None), out_shape=jax.Shap...]
    unnamed x1 -> x0, local copies, waits for them, and re-layouts: 1.28 us -> none
    pallas_call x1, Pallas kernels: 58.1 us -> 57.3 us  [shards(): pl.pallas_call(functools.partial(kernel, None), out_shape=jax.ShapeDtypeS...]
where the time goes in v6:
time: 58.8 us; the launch traced here: 58.6 us
  Pallas kernels  57.3 us (97%)
  other arithmetic  1.29 us (2%)
    pallas_call x1, Pallas kernels, shards(): pl.pallas_call(functools.partial(kernel, None), out_shape=jax.ShapeDtypeS...  57.3 us
    convert_element_type x1, other arithmetic, shards(): return pl.pallas_call(functools.partial(kernel, None), out_shape=jax.Shap...  1.29 us

profile of v6, /device:TPU:1, one launch (start us, length us, event | category | flops | bytes accessed | tf_op | source)
XLA Modules:
  0.0 58.6 jit_solution(15883651073511612330)
XLA Ops:
  0.0 57.3 %shard_map.145 = f32[8,256]{1,0:T(8,128)} custom-call(bf16[8,8192]{1,0:T(8,128)(2,1)} %q_h.1, bf16[8,128,512]{2,1,0:T(8,128)(2,1)} %ck_h.1, bf16[8,128,512]{2,1,0:T(8,128)(2,1)} %cv_h.1, bf16[8,512]{1,0:T(8,128)(2,1)} %nk_h.1, bf16[8,512]{1,0:T(8,128)(2,1)} %nv_h.1, s32[8]{0:T(128)} %len_s.1, bf16[64,1024]{1,0:T(8,128)(2,1)} %res_h.1, ...), custom_call_target="tpu_custom_call" | custom-call | tf_op jit(solution)/shard_map/pallas_call | solution.py:571
  57.4 1.3 %convert_element_type.3 = bf16[8,256]{1,0:T(8,128)(2,1)} convert(f32[8,256]{1,0:T(8,128)} %shard_map.145) | non-fusion elementwise | flops 2048 | bytes 12288 | tf_op jit(solution)/shard_map/convert_element_type | solution.py:597

commit v7 on v6

--- a/solution.py
+++ b/solution.py
@@ -22,7 +22,7 @@
 PARTS = ((0, 3), (3, 6), (6, 8))
 Z_ALL = Z_FAR + (0,)
 RING = (0, 1, 7, 2, 6, 3, 5, 4)
-RUNS = ((0, 3), (3, 8))
+RUNS = ((0, 4), (4, 8))
 PLANE = tuple((dx, dc, dy) for dx in (2, 1, 3, 0) for dy in (2, 1, 3, 0) for dc in (1, 0) if dx or dc or dy)
 YZ_FAR = tuple((dy, dz) for dz in Z_FAR + (0,) for dy in (2, 1, 3, 0) if dy or dz)
 HALF_FAR = tuple((dx, dc, dh) for dh in (1, 0) for dx in (2, 1, 3, 0) for dc in (1, 0) if dx or dc or dh)
@@ -332,7 +332,7 @@
         for at in range(max(lo, 1), hi):
             ref = xs.at[req, at, rows_y]
             rcopy(ref, ref, sz_s.at[at], sz_r.at[at], me).wait_recv()
-        for o in XY_COLUMN:
+        for o in XY_FAR:
             xy_copy(g, *o).start()
         if g == 0:
             drain()

time: 58.8 us -> 58.7 us (level)
  no operation moved by 1% of the time
where the time goes in v7:
time: 58.7 us; the launch traced here: 58.6 us
  Pallas kernels  57.3 us (98%)
  other arithmetic  1.29 us (2%)
    pallas_call x1, Pallas kernels, shards(): pl.pallas_call(functools.partial(kernel, None), out_shape=jax.ShapeDtypeS...  57.3 us
    convert_element_type x1, other arithmetic, shards(): return pl.pallas_call(functools.partial(kernel, None), out_shape=jax.Shap...  1.29 us

profile of v7, /device:TPU:1, one launch (start us, length us, event | category | flops | bytes accessed | tf_op | source)
XLA Modules:
  0.0 58.6 jit_solution(17720479367978611572)
XLA Ops:
  0.0 57.3 %shard_map.145 = f32[8,256]{1,0:T(8,128)} custom-call(bf16[8,8192]{1,0:T(8,128)(2,1)} %q_h.1, bf16[8,128,512]{2,1,0:T(8,128)(2,1)} %ck_h.1, bf16[8,128,512]{2,1,0:T(8,128)(2,1)} %cv_h.1, bf16[8,512]{1,0:T(8,128)(2,1)} %nk_h.1, bf16[8,512]{1,0:T(8,128)(2,1)} %nv_h.1, s32[8]{0:T(128)} %len_s.1, bf16[64,1024]{1,0:T(8,128)(2,1)} %res_h.1, ...), custom_call_target="tpu_custom_call" | custom-call | tf_op jit(solution)/shard_map/pallas_call | solution.py:571
  57.3 1.3 %convert_element_type.3 = bf16[8,256]{1,0:T(8,128)(2,1)} convert(f32[8,256]{1,0:T(8,128)} %shard_map.145) | non-fusion elementwise | flops 2048 | bytes 12288 | tf_op jit(solution)/shard_map/convert_element_type | solution.py:597

commit v8 on v7

--- a/solution.py
+++ b/solution.py
@@ -113,7 +113,7 @@
         pltpu.make_async_copy(wu_h, wgu_v.at[:, pl.ds(128, 128)], lsem.at[11]),
         pltpu.make_async_copy(wd_h, wd_v, lsem.at[12]),
     ]
-    for i in (0, 1, 3, 2, 4, 5, 6, 7, 8, 9, 10, 11, 12):
+    for i in (0, 1, 3, 2, 4):
         local[i].start()
 
     factor = 1.0 / math.sqrt(HD)
@@ -187,6 +187,8 @@
             drains.append(lambda n=n, o=o: acc_copy(n, o).wait_send())
     for j in range(2):
         racc[z, j] = acc_s[j, z]
+    for i in range(5, 13):
+        local[i].start()
 
     def wait_stat(o):
         c = lax.rem(z + o, 8)

time: 58.7 us -> 58.7 us (level)
  no operation moved by 1% of the time
where the time goes in v8:
time: 58.7 us; the launch traced here: 58.6 us
  Pallas kernels  57.3 us (98%)
  other arithmetic  1.29 us (2%)
    pallas_call x1, Pallas kernels, shards(): pl.pallas_call(functools.partial(kernel, None), out_shape=jax.ShapeDtypeS...  57.3 us
    convert_element_type x1, other arithmetic, shards(): return pl.pallas_call(functools.partial(kernel, None), out_shape=jax.Shap...  1.29 us

profile of v8, /device:TPU:1, one launch (start us, length us, event | category | flops | bytes accessed | tf_op | source)
XLA Modules:
  0.0 58.6 jit_solution(10109583490064197442)
XLA Ops:
  0.0 57.3 %shard_map.145 = f32[8,256]{1,0:T(8,128)} custom-call(bf16[8,8192]{1,0:T(8,128)(2,1)} %q_h.1, bf16[8,128,512]{2,1,0:T(8,128)(2,1)} %ck_h.1, bf16[8,128,512]{2,1,0:T(8,128)(2,1)} %cv_h.1, bf16[8,512]{1,0:T(8,128)(2,1)} %nk_h.1, bf16[8,512]{1,0:T(8,128)(2,1)} %nv_h.1, s32[8]{0:T(128)} %len_s.1, bf16[64,1024]{1,0:T(8,128)(2,1)} %res_h.1, ...), custom_call_target="tpu_custom_call" | custom-call | tf_op jit(solution)/shard_map/pallas_call | solution.py:573
  57.3 1.3 %convert_element_type.3 = bf16[8,256]{1,0:T(8,128)(2,1)} convert(f32[8,256]{1,0:T(8,128)} %shard_map.145) | non-fusion elementwise | flops 2048 | bytes 12288 | tf_op jit(solution)/shard_map/convert_element_type | solution.py:599
